TPU v7x, 32 devices: a whole 2x2x4 slice. The times are simulated.
32 devices in a mesh: section: 2 (over core), dp: 16 (over z, y, x).
Axes of the slice: x: 2, y: 2, z: 4, core: 2. Of those that a mesh axis runs over, the one named last changes fastest.
Arguments:
- tokens: bfloat16 [2, 16, 512, 1024], P(None, 'dp'), may hold values from -6 to 6
- segment_ids: int32 [2, 16, 512], P(None, 'dp'), may hold values from 0 to 63, as said below
- row_lengths: int32 [2, 16], P(None, 'dp'), may hold values from 256 to 512, as said below
- w_qkv: bfloat16 [2, 1024, 3072], P('section', 'dp'), may hold values from -0.1875 to 0.1875
- w_out: bfloat16 [2, 1024, 1024], P('section', 'dp'), may hold values from -1 to 1
- w_in: bfloat16 [2, 1024, 4096], P('section', 'dp'), may hold values from -0.1875 to 0.1875
- w_ffn_out: bfloat16 [2, 4096, 1024], P('section', 'dp'), may hold values from -0.09375 to 0.09375
- bias_q: float32 [2, 1024], P('section'), may hold values from -1.75 to 1.75
- bias_v: float32 [2, 1024], P('section'), may hold values from -0.3125 to 0.3125
- bias_out: float32 [2, 1024], P('section'), may hold values from -1.75 to 1.75
- bias_in: float32 [2, 4096], P('section'), may hold values from -1.75 to 1.75
- bias_ffn_out: float32 [2, 1024], P('section'), may hold values from -1.75 to 1.75
- ln_gain: float32 [2, 2, 1024], P('section'), may hold values from 0.25 to 1.75
- ln_shift: float32 [2, 2, 1024], P('section'), may hold values from -1.75 to 1.75
- out_cotangent: bfloat16 [2, 16, 512, 1024], P(None, 'dp'), may hold values from -6 to 6
Outputs:
- layer_out: bfloat16 [2, 2, 16, 512, 1024], P('section', None, 'dp')
- input_grad: bfloat16 [2, 2, 16, 512, 1024], P('section', None, 'dp')
- grad_bias_q: float32 [2, 1024], P('section')
- grad_bias_v: float32 [2, 1024], P('section')
- grad_bias_out: float32 [2, 1024], P('section')
- grad_bias_in: float32 [2, 4096], P('section')
- grad_bias_ffn_out: float32 [2, 1024], P('section')
Inputs may be any that keep to these rules, and one draw needn't show every extreme that they name: `segment_ids`: in each row the numbers start at 0 and never fall along the row; a run of equal numbers is one packed item. `row_lengths`: some row of every draw is full.
All inputs are finite; a program needn't handle non-finite values.
Results may differ from a plain program's by a relative error of at most 0.02.
Values may be sent and summed in bfloat16 or wider, within the bound.
A program may use at most 112 MiB of HBM per device.

v0:
```python
from functools import partial
import math

import jax
import jax.numpy as jnp
from jax import lax
from jax.sharding import PartitionSpec as P

HEADS = 16
HEAD_DIM = 64


epsilon = 1e-06


def shifted(array, axis, by):
    count = lax.axis_size(axis)
    pairs = [(i, i + by) for i in range(count) if 0 <= i + by < count]
    return lax.ppermute(array, axis, pairs)


def rounded(values):
    return lax.optimization_barrier(values.astype(jnp.bfloat16))


def transposed(left, matrix):
    return lax.dot_general(
        left, matrix, (((1,), (1,)), ((), ())), preferred_element_type=jnp.float32
    )


def layer_norm(residual):
    average = jnp.mean(residual, -1, keepdims=True)
    centered = residual - average
    inverse = lax.rsqrt(jnp.mean(centered * centered, -1, keepdims=True) + epsilon)
    return (centered * inverse, inverse)


def norm_back(upstream, normed, inverse):
    return inverse * (
        upstream
        - jnp.mean(upstream, -1, keepdims=True)
        - normed * jnp.mean(upstream * normed, -1, keepdims=True)
    )


def pair_mask(segments, length):
    positions = jnp.arange(segments.shape[0], dtype=jnp.int32)
    is_valid = positions < length
    return (segments[:, None] == segments[None, :]) & (is_valid[:, None] == is_valid[None, :])


def masked_scores(queries, key_rows, allowed):
    scale_factor = 1.0 / math.sqrt(queries.shape[-1])
    scores = (
        jnp.einsum("qhd,khd->hqk", queries, key_rows, preferred_element_type=jnp.float32)
        * scale_factor
    )
    return jnp.where(allowed[None], scores, -1000000000.0)


def attend_row(scanned):
    queries, key_rows, values, segments, length = scanned
    scores = masked_scores(queries, key_rows, pair_mask(segments, length))
    row_max = jnp.max(scores, -1, keepdims=True)
    exp_scores = jnp.exp(scores - row_max)
    totals = jnp.sum(exp_scores, -1, keepdims=True)
    probs_low = (exp_scores / totals).astype(jnp.bfloat16)
    context = jnp.einsum("hqk,khd->qhd", probs_low, values, preferred_element_type=jnp.float32)
    return (context.astype(jnp.bfloat16), row_max + jnp.log(totals))


def attend_back(scanned):
    queries, key_rows, values, log_total, grad_context, segments, length = scanned
    scores = masked_scores(queries, key_rows, pair_mask(segments, length))
    attn_probs = jnp.exp(scores - log_total)
    grad_probs = jnp.einsum(
        "qhd,khd->hqk", grad_context, values, preferred_element_type=jnp.float32
    )
    grad_values = jnp.einsum(
        "hqk,qhd->khd",
        attn_probs.astype(jnp.bfloat16),
        grad_context,
        preferred_element_type=jnp.float32,
    )
    delta_rows = jnp.sum(attn_probs * grad_probs, -1, keepdims=True)
    grad_scores = (attn_probs * (grad_probs - delta_rows)).astype(jnp.bfloat16)
    scale_factor = 1.0 / math.sqrt(queries.shape[-1])
    grad_queries = (
        jnp.einsum("hqk,khd->qhd", grad_scores, key_rows, preferred_element_type=jnp.float32)
        * scale_factor
    )
    grad_keys = (
        jnp.einsum("hqk,qhd->khd", grad_scores, queries, preferred_element_type=jnp.float32)
        * scale_factor
    )
    return jnp.stack([grad_queries, grad_keys, grad_values], 1)


def layer_forward(inputs, matrices, params, segments, lengths):
    mat_qkv, mat_attn, mat_hidden, mat_final = matrices
    bias_query, bias_value, bias_attn, bias_hidden, bias_final, gain_rows, shifts = params
    row_count, seq_len, model_width = inputs.shape
    flat_rows = inputs.reshape(row_count * seq_len, model_width)
    projected = jnp.dot(flat_rows, mat_qkv, preferred_element_type=jnp.float32)
    projected = projected + jnp.concatenate([bias_query, jnp.zeros_like(bias_query), bias_value])
    projected = projected.astype(jnp.bfloat16).reshape(row_count, seq_len, 3, HEADS, HEAD_DIM)
    queries = projected[:, :, 0]
    key_rows = projected[:, :, 1]
    values = projected[:, :, 2]
    context, log_total = lax.map(attend_row, (queries, key_rows, values, segments, lengths))
    attn_out = (
        jnp.dot(
            context.reshape(row_count * seq_len, model_width),
            mat_attn,
            preferred_element_type=jnp.float32,
        )
        + bias_attn
    )
    normed_first, inv_first = layer_norm(flat_rows.astype(jnp.float32) + attn_out)
    hidden = rounded(normed_first * gain_rows[0] + shifts[0])
    pre_gelu = jnp.dot(hidden, mat_hidden, preferred_element_type=jnp.float32) + bias_hidden
    activated = jax.nn.gelu(pre_gelu, approximate=False).astype(jnp.bfloat16)
    residual = (
        hidden.astype(jnp.float32)
        + jnp.dot(activated, mat_final, preferred_element_type=jnp.float32)
        + bias_final
    )
    normed_second, inv_second = layer_norm(residual)
    output = normed_second * gain_rows[1] + shifts[1]
    stored = (
        queries,
        key_rows,
        values,
        log_total,
        normed_first,
        inv_first,
        pre_gelu,
        normed_second,
        inv_second,
    )
    return (output, stored)


def layer_backward(inputs, grad_out, matrices, params, segments, lengths):
    mat_qkv, mat_attn, mat_hidden, mat_final = matrices
    gain_rows = params[5]
    _, stored = layer_forward(inputs, matrices, params, segments, lengths)
    (
        queries,
        key_rows,
        values,
        log_total,
        normed_first,
        inv_first,
        pre_gelu,
        normed_second,
        inv_second,
    ) = stored
    model_width = inputs.shape[-1]
    grad_flat = grad_out.reshape(-1, model_width)
    grad_second = norm_back(grad_flat * gain_rows[1], normed_second, inv_second)
    grad_ffn = rounded(grad_second)
    grad_act = transposed(grad_ffn, mat_final)
    _, gelu_back = jax.vjp(partial(jax.nn.gelu, approximate=False), pre_gelu)
    grad_pre = rounded(gelu_back(grad_act)[0])
    grad_hidden = rounded(grad_second + transposed(grad_pre, mat_hidden)).astype(jnp.float32)
    grad_first = norm_back(grad_hidden * gain_rows[0], normed_first, inv_first)
    grad_attn = rounded(grad_first)
    grad_context = transposed(grad_attn, mat_attn).astype(jnp.bfloat16).reshape(queries.shape)
    grad_proj = lax.map(
        attend_back, (queries, key_rows, values, log_total, grad_context, segments, lengths)
    )
    grad_proj = rounded(grad_proj.reshape(-1, 3 * model_width))
    grad_inputs = grad_first + transposed(grad_proj, mat_qkv)
    proj_sums = jnp.sum(grad_proj.astype(jnp.float32), 0)
    bias_terms = (
        proj_sums[:model_width],
        proj_sums[2 * model_width :],
        jnp.sum(grad_attn.astype(jnp.float32), 0),
        jnp.sum(grad_pre.astype(jnp.float32), 0),
        jnp.sum(grad_ffn.astype(jnp.float32), 0),
    )
    return (grad_inputs.astype(jnp.bfloat16).reshape(inputs.shape), bias_terms)


def on_device(
    tokens,
    segment_ids,
    row_lengths,
    w_qkv,
    w_out,
    w_in,
    w_ffn_out,
    bias_q,
    bias_v,
    bias_out,
    bias_in,
    bias_ffn_out,
    ln_gain,
    ln_shift,
    out_cotangent,
):
    micro_count = tokens.shape[0]
    leading = lax.axis_index("section") == 0
    params = (
        bias_q[0],
        bias_v[0],
        bias_out[0],
        bias_in[0],
        bias_ffn_out[0],
        ln_gain[0],
        ln_shift[0],
    )

    def forward_step(incoming, tick_index):
        gathered_now = (
            lax.all_gather(w_qkv, "dp", axis=1, tiled=True),
            lax.all_gather(w_out, "dp", axis=1, tiled=True),
            lax.all_gather(w_in, "dp", axis=1, tiled=True),
            lax.all_gather(w_ffn_out, "dp", axis=1, tiled=True),
        )
        matrices = tuple((matrix[0] for matrix in gathered_now))
        own_input = lax.dynamic_index_in_dim(
            tokens, jnp.minimum(tick_index, micro_count - 1), 0, keepdims=False
        )
        current = jnp.where(leading, own_input, incoming)
        micro_index = jnp.clip(jnp.where(leading, tick_index, tick_index - 1), 0, micro_count - 1)
        segments = lax.dynamic_index_in_dim(segment_ids, micro_index, 0, keepdims=False)
        lengths = lax.dynamic_index_in_dim(row_lengths, micro_index, 0, keepdims=False)
        is_live = jnp.where(leading, tick_index < micro_count, tick_index >= 1)

        def forward_compute():
            output, _ = layer_forward(current, matrices, params, segments, lengths)
            return output.astype(jnp.bfloat16).reshape(current.shape)

        def forward_empty_fill():
            return jnp.zeros_like(current)

        result = lax.cond(is_live, forward_compute, forward_empty_fill)
        handed = shifted(result, "section", 1)
        return (handed, (current, result))

    tick_steps = jnp.arange(micro_count + 1, dtype=jnp.int32)
    _, (section_inputs, section_outputs) = lax.scan(
        forward_step, jnp.zeros_like(tokens[0]), tick_steps
    )

    def backward_step(carried, scanned):
        incoming, totals = carried
        tick_index, current = scanned
        gathered_now = (
            lax.all_gather(w_qkv, "dp", axis=1, tiled=True),
            lax.all_gather(w_out, "dp", axis=1, tiled=True),
            lax.all_gather(w_in, "dp", axis=1, tiled=True),
            lax.all_gather(w_ffn_out, "dp", axis=1, tiled=True),
        )
        matrices = tuple((matrix[0] for matrix in gathered_now))
        own_cot = lax.dynamic_index_in_dim(
            out_cotangent,
            jnp.clip(micro_count - 1 - tick_index, 0, micro_count - 1),
            0,
            keepdims=False,
        )
        grad_here = jnp.where(leading, incoming, own_cot)
        micro_index = jnp.clip(
            jnp.where(leading, micro_count - tick_index, micro_count - 1 - tick_index),
            0,
            micro_count - 1,
        )
        segments = lax.dynamic_index_in_dim(segment_ids, micro_index, 0, keepdims=False)
        lengths = lax.dynamic_index_in_dim(row_lengths, micro_index, 0, keepdims=False)
        is_live = jnp.where(leading, tick_index >= 1, tick_index < micro_count)

        def backward_compute():
            return layer_backward(
                current, grad_here.astype(jnp.float32), matrices, params, segments, lengths
            )

        def backward_empty_fill():
            return (jnp.zeros_like(current), tuple((jnp.zeros_like(total) for total in totals)))

        grad_in, bias_terms = lax.cond(is_live, backward_compute, backward_empty_fill)
        handed = shifted(grad_in, "section", -1)
        bias_terms = lax.psum(bias_terms, "dp")
        totals = tuple((running + update for running, update in zip(totals, bias_terms)))
        return ((handed, totals), grad_in)

    model_width = tokens.shape[-1]
    hidden_width = bias_in.shape[-1]
    zero_sums = (
        jnp.zeros((model_width,), jnp.float32),
        jnp.zeros((model_width,), jnp.float32),
        jnp.zeros((model_width,), jnp.float32),
        jnp.zeros((hidden_width,), jnp.float32),
        jnp.zeros((model_width,), jnp.float32),
    )
    (_, totals), grad_inputs = lax.scan(
        backward_step, (jnp.zeros_like(tokens[0]), zero_sums), (tick_steps, section_inputs[::-1])
    )
    layer_out = jnp.where(leading, section_outputs[:micro_count], section_outputs[1:])[None]
    input_grad = jnp.where(leading, grad_inputs[1:][::-1], grad_inputs[:micro_count][::-1])[None]
    return (
        layer_out,
        input_grad,
        totals[0][None],
        totals[1][None],
        totals[2][None],
        totals[3][None],
        totals[4][None],
    )


def solution(mesh):
    placed = (
        P(None, "dp", None, None),
        P(None, "dp", None),
        P(None, "dp"),
        P("section", "dp", None),
        P("section", "dp", None),
        P("section", "dp", None),
        P("section", "dp", None),
        P("section", None),
        P("section", None),
        P("section", None),
        P("section", None),
        P("section", None),
        P("section", None, None),
        P("section", None, None),
        P(None, "dp", None, None),
    )
    return jax.shard_map(
        on_device,
        mesh=mesh,
        in_specs=placed,
        out_specs=(
            P("section", None, "dp", None, None),
            P("section", None, "dp", None, None),
            P("section", None),
            P("section", None),
            P("section", None),
            P("section", None),
            P("section", None),
        ),
        check_vma=False,
    )
```

profile of v0, /device:TPU:0, one launch (start us, length us, event | category | flops | bytes accessed | tf_op | source)
XLA Modules:
  0.0 3283.7 jit_solution(10165588233442264448)
XLA Ops:
  12.0 1388.5 %while.36 = (s32[]{:T(128)}, bf16[1,512,1024]{2,1,0:T(8,128)(2,1)S(1)}, bf16[3,1,512,1024]{3,2,1,0:T(8,128)(2,1)}, bf16[3,1,512,1024]{3,2,1,0:T(8,128)(2,1)}, s3...) while((s32[]{:T(128)}, ...), condition=%wide.region_9.10_spmd, body=%wide.region_0.9_spmd.sunk | while | flops 14142415872 | bytes 194322768 | solution.py:245
  79.0 95.6 %all-gather.9.cloned.1.call-done = bf16[1,1024,3072]{2,1,0:T(8,128)(2,1)} async-done(((bf16[1,64,3072]{2,1,0:T(8,128)(2,1)}), bf16[1,1024,3072]{2,1,0:T(8,128)(2,1)}) %all-gather.9.cloned.1.call-update) | async-done | bytes 6291472 | tf_op jit(solution)/shard_map/while/body/eval_jaxpr/all_gather | solution.py:218
  174.6 113.9 %all-gather.15.cloned.1.call-done = bf16[1,4096,1024]{2,1,0:T(8,128)(2,1)} async-done(((bf16[1,256,1024]{2,1,0:T(8,128)(2,1)}), bf16[1,4096,1024]{2,1,0:T(8,128)(2,1)}) %all-gather.15.cloned.1.call-update) | async-done | bytes 8388624 | tf_op jit(solution)/shard_map/while/body/eval_jaxpr/all_gather | solution.py:221
  288.5 113.7 %all-gather.13.cloned.1.call-done = bf16[1,1024,4096]{2,1,0:T(8,128)(2,1)} async-done(((bf16[1,64,4096]{2,1,0:T(8,128)(2,1)}), bf16[1,1024,4096]{2,1,0:T(8,128)(2,1)}) %all-gather.13.cloned.1.call-update) | async-done | bytes 8388624 | tf_op jit(solution)/shard_map/while/body/eval_jaxpr/all_gather | solution.py:220
  540.1 95.4 %all-gather.9.cloned.1.call-done = bf16[1,1024,3072]{2,1,0:T(8,128)(2,1)} async-done(((bf16[1,64,3072]{2,1,0:T(8,128)(2,1)}), bf16[1,1024,3072]{2,1,0:T(8,128)(2,1)}) %all-gather.9.cloned.1.call-update) | async-done | bytes 6291472 | tf_op jit(solution)/shard_map/while/body/eval_jaxpr/all_gather | solution.py:218
  635.6 113.9 %all-gather.15.cloned.1.call-done = bf16[1,4096,1024]{2,1,0:T(8,128)(2,1)} async-done(((bf16[1,256,1024]{2,1,0:T(8,128)(2,1)}), bf16[1,4096,1024]{2,1,0:T(8,128)(2,1)}) %all-gather.15.cloned.1.call-update) | async-done | bytes 8388624 | tf_op jit(solution)/shard_map/while/body/eval_jaxpr/all_gather | solution.py:221
  749.5 113.8 %all-gather.13.cloned.1.call-done = bf16[1,1024,4096]{2,1,0:T(8,128)(2,1)} async-done(((bf16[1,64,4096]{2,1,0:T(8,128)(2,1)}), bf16[1,1024,4096]{2,1,0:T(8,128)(2,1)}) %all-gather.13.cloned.1.call-update) | async-done | bytes 8388624 | tf_op jit(solution)/shard_map/while/body/eval_jaxpr/all_gather | solution.py:220
  1002.1 95.4 %all-gather.9.cloned.1.call-done = bf16[1,1024,3072]{2,1,0:T(8,128)(2,1)} async-done(((bf16[1,64,3072]{2,1,0:T(8,128)(2,1)}), bf16[1,1024,3072]{2,1,0:T(8,128)(2,1)}) %all-gather.9.cloned.1.call-update) | async-done | bytes 6291472 | tf_op jit(solution)/shard_map/while/body/eval_jaxpr/all_gather | solution.py:218
  1097.5 113.9 %all-gather.15.cloned.1.call-done = bf16[1,4096,1024]{2,1,0:T(8,128)(2,1)} async-done(((bf16[1,256,1024]{2,1,0:T(8,128)(2,1)}), bf16[1,4096,1024]{2,1,0:T(8,128)(2,1)}) %all-gather.15.cloned.1.call-update) | async-done | bytes 8388624 | tf_op jit(solution)/shard_map/while/body/eval_jaxpr/all_gather | solution.py:221
  1211.5 113.7 %all-gather.13.cloned.1.call-done = bf16[1,1024,4096]{2,1,0:T(8,128)(2,1)} async-done(((bf16[1,64,4096]{2,1,0:T(8,128)(2,1)}), bf16[1,1024,4096]{2,1,0:T(8,128)(2,1)}) %all-gather.13.cloned.1.call-update) | async-done | bytes 8388624 | tf_op jit(solution)/shard_map/while/body/eval_jaxpr/all_gather | solution.py:220
  1407.6 1861.9 %while.37 = (s32[]{:T(128)}, bf16[1,512,1024]{2,1,0:T(8,128)(2,1)}, f32[1024]{0:T(1024)}, f32[1024]{0:T(1024)}, f32[1024]{0:T(1024)}, /*index=5*/f32[4096]{0:T(1...) while((s32[]{:T(128)}, bf16[1,512,1024]{2,1,0:T(8,128)(2,1)}, ...), condition=%wide.region_33.34_spmd.clone, body=%wide.region_10.33_spmd.clone.sunk | while | flops 29292240896 | bytes 513922432 | solution.py:298
  1479.1 95.4 %all-gather.17.cloned.1.call-done = bf16[1,1024,3072]{2,1,0:T(8,128)(2,1)} async-done(((bf16[1,64,3072]{2,1,0:T(8,128)(2,1)}), bf16[1,1024,3072]{2,1,0:T(8,128)(2,1)}) %all-gather.17.cloned.1.call-update) | async-done | bytes 6291472 | tf_op jit(solution)/shard_map/while/body/eval_jaxpr/all_gather | solution.py:253
  1574.5 113.8 %all-gather.23.cloned.1.call-done = bf16[1,4096,1024]{2,1,0:T(8,128)(2,1)} async-done(((bf16[1,256,1024]{2,1,0:T(8,128)(2,1)}), bf16[1,4096,1024]{2,1,0:T(8,128)(2,1)}) %all-gather.23.cloned.1.call-update) | async-done | bytes 8388624 | tf_op jit(solution)/shard_map/while/body/eval_jaxpr/all_gather | solution.py:256
  1688.3 113.7 %all-gather.21.cloned.1.call-done = bf16[1,1024,4096]{2,1,0:T(8,128)(2,1)} async-done(((bf16[1,64,4096]{2,1,0:T(8,128)(2,1)}), bf16[1,1024,4096]{2,1,0:T(8,128)(2,1)}) %all-gather.21.cloned.1.call-update) | async-done | bytes 8388624 | tf_op jit(solution)/shard_map/while/body/eval_jaxpr/all_gather | solution.py:255
  1885.2 78.1 %collective-permute-done.1 = bf16[1,512,1024]{2,1,0:T(8,128)(2,1)S(1)} collective-permute-done((bf16[1,512,1024]{2,1,0:T(8,128)(2,1)}, bf16[1,512,1024]{2,1,0:T(8,128)(2,1)S(1)}, u32[]{:S(2)}, u32[]{:S(2)}) %collective-permute-start.1) | collective-permute-done | bytes 1048608 | tf_op jit(solution)/shard_map/while/body/eval_jaxpr/ppermute | solution.py:19
  1969.2 116.0 %all-gather.19.cloned.1.call-done = bf16[1,1024,1024]{2,1,0:T(8,128)(2,1)} async-done(((bf16[1,64,1024]{2,1,0:T(8,128)(2,1)}), bf16[1,1024,1024]{2,1,0:T(8,128)(2,1)}) %all-gather.19.cloned.1.call-update) | async-done | bytes 2097168 | tf_op jit(solution)/shard_map/while/body/eval_jaxpr/all_gather | solution.py:254
  2085.2 95.4 %all-gather.17.cloned.1.call-done = bf16[1,1024,3072]{2,1,0:T(8,128)(2,1)} async-done(((bf16[1,64,3072]{2,1,0:T(8,128)(2,1)}), bf16[1,1024,3072]{2,1,0:T(8,128)(2,1)}) %all-gather.17.cloned.1.call-update) | async-done | bytes 6291472 | tf_op jit(solution)/shard_map/while/body/eval_jaxpr/all_gather | solution.py:253
  2180.7 113.9 %all-gather.23.cloned.1.call-done = bf16[1,4096,1024]{2,1,0:T(8,128)(2,1)} async-done(((bf16[1,256,1024]{2,1,0:T(8,128)(2,1)}), bf16[1,4096,1024]{2,1,0:T(8,128)(2,1)}) %all-gather.23.cloned.1.call-update) | async-done | bytes 8388624 | tf_op jit(solution)/shard_map/while/body/eval_jaxpr/all_gather | solution.py:256
  2294.6 113.7 %all-gather.21.cloned.1.call-done = bf16[1,1024,4096]{2,1,0:T(8,128)(2,1)} async-done(((bf16[1,64,4096]{2,1,0:T(8,128)(2,1)}), bf16[1,1024,4096]{2,1,0:T(8,128)(2,1)}) %all-gather.21.cloned.1.call-update) | async-done | bytes 8388624 | tf_op jit(solution)/shard_map/while/body/eval_jaxpr/all_gather | solution.py:255
  2408.3 158.7 %conditional.6 = (bf16[1,512,1024]{2,1,0:T(8,128)(2,1)}, f32[1024]{0:T(1024)S(1)}, f32[1024]{0:T(1024)S(1)}, f32[1024]{0:T(1024)}, f32[4096]{0:T(1024)}, /*index...) conditional(s32[]{:T(128)} %convert_element_type.290, () %tuple.127, (bf16[3,1,512,1024]{3,2,1,0:T(8,128)(2,1)}, ...), branch_computations={%region_11.11_spmd, %region_12.27_spmd} | conditional | flops 29292216320 | bytes 422793120 | solution.py:283
  2706.0 95.6 %all-gather.17.cloned.1.call-done = bf16[1,1024,3072]{2,1,0:T(8,128)(2,1)} async-done(((bf16[1,64,3072]{2,1,0:T(8,128)(2,1)}), bf16[1,1024,3072]{2,1,0:T(8,128)(2,1)}) %all-gather.17.cloned.1.call-update) | async-done | bytes 6291472 | tf_op jit(solution)/shard_map/while/body/eval_jaxpr/all_gather | solution.py:253
  2801.6 113.9 %all-gather.23.cloned.1.call-done = bf16[1,4096,1024]{2,1,0:T(8,128)(2,1)} async-done(((bf16[1,256,1024]{2,1,0:T(8,128)(2,1)}), bf16[1,4096,1024]{2,1,0:T(8,128)(2,1)}) %all-gather.23.cloned.1.call-update) | async-done | bytes 8388624 | tf_op jit(solution)/shard_map/while/body/eval_jaxpr/all_gather | solution.py:256
  2915.6 113.7 %all-gather.21.cloned.1.call-done = bf16[1,1024,4096]{2,1,0:T(8,128)(2,1)} async-done(((bf16[1,64,4096]{2,1,0:T(8,128)(2,1)}), bf16[1,1024,4096]{2,1,0:T(8,128)(2,1)}) %all-gather.21.cloned.1.call-update) | async-done | bytes 8388624 | tf_op jit(solution)/shard_map/while/body/eval_jaxpr/all_gather | solution.py:255
  3029.2 158.7 %conditional.6 = (bf16[1,512,1024]{2,1,0:T(8,128)(2,1)}, f32[1024]{0:T(1024)S(1)}, f32[1024]{0:T(1024)S(1)}, f32[1024]{0:T(1024)}, f32[4096]{0:T(1024)}, /*index...) conditional(s32[]{:T(128)} %convert_element_type.290, () %tuple.127, (bf16[3,1,512,1024]{3,2,1,0:T(8,128)(2,1)}, ...), branch_computations={%region_11.11_spmd, %region_12.27_spmd} | conditional | flops 29292216320 | bytes 422793120 | solution.py:283
  (381 shorter events, 1259.0 us)
Async XLA Ops:
  12.0 67.0 %all-gather.11.cloned.1.call-start = ((), (), s32[]{:S(2)}) async-start(), calls=%async_computation.1 | async-start | bytes 2228224 | tf_op jit(solution)/shard_map/while/body/eval_jaxpr/all_gather | solution.py:219
  12.7 161.9 %all-gather.9.cloned.1.call-start = ((), (), s32[]{:S(2)}) async-start(), calls=%async_computation | async-start | bytes 6684672 | tf_op jit(solution)/shard_map/while/body/eval_jaxpr/all_gather | solution.py:218
  13.4 275.1 %all-gather.15.cloned.1.call-start = ((), (), s32[]{:S(2)}) async-start(), calls=%async_computation.3 | async-start | bytes 8912896 | tf_op jit(solution)/shard_map/while/body/eval_jaxpr/all_gather | solution.py:221
  14.2 388.0 %all-gather.13.cloned.1.call-start = ((), (), s32[]{:S(2)}) async-start(), calls=%async_computation.2 | async-start | bytes 8912896 | tf_op jit(solution)/shard_map/while/body/eval_jaxpr/all_gather | solution.py:220
  478.4 157.1 %all-gather.9.cloned.1.call-start = ((), (), s32[]{:S(2)}) async-start(), calls=%async_computation | async-start | bytes 6684672 | tf_op jit(solution)/shard_map/while/body/eval_jaxpr/all_gather | solution.py:218
  479.0 270.4 %all-gather.15.cloned.1.call-start = ((), (), s32[]{:S(2)}) async-start(), calls=%async_computation.3 | async-start | bytes 8912896 | tf_op jit(solution)/shard_map/while/body/eval_jaxpr/all_gather | solution.py:221
  479.8 383.5 %all-gather.13.cloned.1.call-start = ((), (), s32[]{:S(2)}) async-start(), calls=%async_computation.2 | async-start | bytes 8912896 | tf_op jit(solution)/shard_map/while/body/eval_jaxpr/all_gather | solution.py:220
  939.7 157.8 %all-gather.9.cloned.1.call-start = ((), (), s32[]{:S(2)}) async-start(), calls=%async_computation | async-start | bytes 6684672 | tf_op jit(solution)/shard_map/while/body/eval_jaxpr/all_gather | solution.py:218
  940.3 271.2 %all-gather.15.cloned.1.call-start = ((), (), s32[]{:S(2)}) async-start(), calls=%async_computation.3 | async-start | bytes 8912896 | tf_op jit(solution)/shard_map/while/body/eval_jaxpr/all_gather | solution.py:221
  941.0 384.1 %all-gather.13.cloned.1.call-start = ((), (), s32[]{:S(2)}) async-start(), calls=%async_computation.2 | async-start | bytes 8912896 | tf_op jit(solution)/shard_map/while/body/eval_jaxpr/all_gather | solution.py:220
  1327.3 73.2 %collective-permute-start = (bf16[1,512,1024]{2,1,0:T(8,128)(2,1)}, bf16[1,512,1024]{2,1,0:T(8,128)(2,1)S(1)}, u32[]{:S(2)}, u32[]{:S(2)}) collective-permute-start(bf16[1,512,1024]{2,1,0:T(8,128)(2,1)} %get-tuple-element.1434), channel_id=1, source_target_pairs={{0,16},{1,17},{2,18},{3,19},{4,20},{5,21},{6,22},{7,23},{8,24},{9,... | collective-permute-start | bytes 3145736 | tf_op jit(solution)/shard_map/while/body/eval_jaxpr/ppermute | solution.py:19
  1416.4 158.1 %all-gather.17.cloned.1.call-start = ((), (), s32[]{:S(2)}) async-start(), calls=%async_computation.4 | async-start | bytes 6684672 | tf_op jit(solution)/shard_map/while/body/eval_jaxpr/all_gather | solution.py:253
  1417.0 271.3 %all-gather.23.cloned.1.call-start = ((), (), s32[]{:S(2)}) async-start(), calls=%async_computation.7 | async-start | bytes 8912896 | tf_op jit(solution)/shard_map/while/body/eval_jaxpr/all_gather | solution.py:256
  1417.5 384.4 %all-gather.21.cloned.1.call-start = ((), (), s32[]{:S(2)}) async-start(), calls=%async_computation.6 | async-start | bytes 8912896 | tf_op jit(solution)/shard_map/while/body/eval_jaxpr/all_gather | solution.py:255
  1807.5 155.8 %collective-permute-start.1 = (bf16[1,512,1024]{2,1,0:T(8,128)(2,1)}, bf16[1,512,1024]{2,1,0:T(8,128)(2,1)S(1)}, u32[]{:S(2)}, u32[]{:S(2)}) collective-permute-start(bf16[1,512,1024]{2,1,0:T(8,128)(2,1)} %get-tuple-element.1462), channel_id=1, source_target_pairs={{16,0},{17,1},{18,2},{19,3},{20,4},{21,5},{22,6},{23,7},{24,8},{25... | collective-permute-start | bytes 3145736 | tf_op jit(solution)/shard_map/while/body/eval_jaxpr/ppermute | solution.py:19
  1964.3 120.9 %all-gather.19.cloned.1.call-start = ((), (), s32[]{:S(2)}) async-start(), calls=%async_computation.5 | async-start | bytes 2228224 | tf_op jit(solution)/shard_map/while/body/eval_jaxpr/all_gather | solution.py:254
  1964.9 215.8 %all-gather.17.cloned.1.call-start = ((), (), s32[]{:S(2)}) async-start(), calls=%async_computation.4 | async-start | bytes 6684672 | tf_op jit(solution)/shard_map/while/body/eval_jaxpr/all_gather | solution.py:253
  1965.5 329.1 %all-gather.23.cloned.1.call-start = ((), (), s32[]{:S(2)}) async-start(), calls=%async_computation.7 | async-start | bytes 8912896 | tf_op jit(solution)/shard_map/while/body/eval_jaxpr/all_gather | solution.py:256
  1966.2 442.0 %all-gather.21.cloned.1.call-start = ((), (), s32[]{:S(2)}) async-start(), calls=%async_computation.6 | async-start | bytes 8912896 | tf_op jit(solution)/shard_map/while/body/eval_jaxpr/all_gather | solution.py:255
  2566.9 77.7 %collective-permute-start.1 = (bf16[1,512,1024]{2,1,0:T(8,128)(2,1)}, bf16[1,512,1024]{2,1,0:T(8,128)(2,1)S(1)}, u32[]{:S(2)}, u32[]{:S(2)}) collective-permute-start(bf16[1,512,1024]{2,1,0:T(8,128)(2,1)} %get-tuple-element.1462), channel_id=1, source_target_pairs={{16,0},{17,1},{18,2},{19,3},{20,4},{21,5},{22,6},{23,7},{24,8},{25... | collective-permute-start | bytes 3145736 | tf_op jit(solution)/shard_map/while/body/eval_jaxpr/ppermute | solution.py:19
  2646.6 155.1 %all-gather.17.cloned.1.call-start = ((), (), s32[]{:S(2)}) async-start(), calls=%async_computation.4 | async-start | bytes 6684672 | tf_op jit(solution)/shard_map/while/body/eval_jaxpr/all_gather | solution.py:253
  2647.3 268.2 %all-gather.23.cloned.1.call-start = ((), (), s32[]{:S(2)}) async-start(), calls=%async_computation.7 | async-start | bytes 8912896 | tf_op jit(solution)/shard_map/while/body/eval_jaxpr/all_gather | solution.py:256
  2648.0 381.2 %all-gather.21.cloned.1.call-start = ((), (), s32[]{:S(2)}) async-start(), calls=%async_computation.6 | async-start | bytes 8912896 | tf_op jit(solution)/shard_map/while/body/eval_jaxpr/all_gather | solution.py:255
  3188.0 77.7 %collective-permute-start.1 = (bf16[1,512,1024]{2,1,0:T(8,128)(2,1)}, bf16[1,512,1024]{2,1,0:T(8,128)(2,1)S(1)}, u32[]{:S(2)}, u32[]{:S(2)}) collective-permute-start(bf16[1,512,1024]{2,1,0:T(8,128)(2,1)} %get-tuple-element.1462), channel_id=1, source_target_pairs={{16,0},{17,1},{18,2},{19,3},{20,4},{21,5},{22,6},{23,7},{24,8},{25... | collective-permute-start | bytes 3145736 | tf_op jit(solution)/shard_map/while/body/eval_jaxpr/ppermute | solution.py:19
  (67 other events, 3628.6 us)
Sparse Core Ops, SparseCore 0:
  15.6 63.3 all-gather.10
  81.8 92.7 all-gather.8
  177.4 111.0 all-gather.14
  291.1 111.0 all-gather.12
  481.2 58.9 all-gather.10
  542.7 92.7 all-gather.8
  638.3 111.0 all-gather.14
  752.2 111.0 all-gather.12
  942.6 59.4 all-gather.10
  1004.7 92.7 all-gather.8
  1100.3 111.0 all-gather.14
  1214.1 111.0 all-gather.12
  1419.2 59.7 all-gather.18
  1481.7 92.7 all-gather.16
  1577.1 111.0 all-gather.22
  1690.9 111.0 all-gather.20
  1967.6 117.5 all-gather.18
  2087.8 92.7 all-gather.16
  2183.4 111.0 all-gather.22
  2297.2 111.0 all-gather.20
  2649.4 56.5 all-gather.18
  2708.8 92.7 all-gather.16
  2804.4 111.0 all-gather.22
  2918.2 111.0 all-gather.20
where the time goes:
time: 3310 us; the launch traced here: 3280 us
  waiting for transfers between devices  2430 us (73%)
  matrix products  349 us (11%)
  blocking collectives  222 us (7%)
  other arithmetic  82.4 us (2%)
  local copies, waits for them, and re-layouts  79.8 us (2%)
  starting transfers between devices  78.1 us (2%)
    all_gather x3, waiting for transfers between devices, forward_step(): lax.all_gather(w_ffn_out, 'dp', axis=1, tiled=True)  342 us
    all_gather x3, waiting for transfers between devices, backward_step(): lax.all_gather(w_ffn_out, 'dp', axis=1, tiled=True)  342 us
    all_gather x3, waiting for transfers between devices, forward_step(): lax.all_gather(w_in, 'dp', axis=1, tiled=True)  341 us
    all_gather x3, waiting for transfers between devices, backward_step(): lax.all_gather(w_in, 'dp', axis=1, tiled=True)  341 us
    all_gather x3, waiting for transfers between devices, backward_step(): lax.all_gather(w_qkv, 'dp', axis=1, tiled=True)  286 us
    all_gather x3, waiting for transfers between devices, forward_step(): lax.all_gather(w_qkv, 'dp', axis=1, tiled=True)  286 us
    all_gather x3, waiting for transfers between devices, backward_step(): lax.all_gather(w_out, 'dp', axis=1, tiled=True)  230 us
    psum x3, blocking collectives, backward_step(): bias_terms = lax.psum(bias_terms, 'dp')  222 us
  transfers between devices with their start and end apart: 30, of which 28 were waited for; matrix products, arithmetic and copies ran while one was open for 1% of the time, Pallas kernels for 0%

commit v1 on v0

v1 whole, which is shorter than its diff:
```python
from functools import partial
import math

import jax
import jax.numpy as jnp
from jax import lax
from jax.experimental import pallas as pl
from jax.experimental.pallas import tpu as pltpu
from jax.sharding import PartitionSpec as P

HEAD_DIM = 64
SEQ = 512
epsilon = 1e-06
VMEM_LIMIT = 60 * 2**20

MESH = pl.DeviceIdType.MESH
LANES = 1024
BLOCK = 64
HALF = BLOCK // 2
CUT = 384
STAGES = (0, 1, 2, 3, 4, 6)


LOAD = 7


def link_plan(
    items, wq, wo, wi, wf, own_vec, full, vec, vec_sem, stage, in_sem, place_sem, cross_send, cross_recv, send_sem, recv_sem
):
    sec = lax.axis_index("section")
    chip = lax.axis_index("dp")
    z = chip // 4
    y = (chip // 2) % 2
    x = chip % 2
    dev_x = (sec, z * 4 + y * 2 + 1 - x)
    dev_y = (sec, z * 4 + (1 - y) * 2 + x)
    dev_up = (sec, jnp.minimum(z + 1, 3) * 4 + y * 2 + x)
    dev_down = (sec, jnp.maximum(z - 1, 0) * 4 + y * 2 + x)
    dev_core = (1 - sec, chip)
    per_layer = items // 2

    def own_block(b, row):
        if b < 3:
            return wq.at[0, pl.ds(row, HALF), b * LANES : (b + 1) * LANES]
        if b == 3:
            return wo.at[0, pl.ds(row, HALF), :]
        if b < 8:
            return wi.at[0, pl.ds(row, HALF), (b - 4) * LANES : (b - 3) * LANES]
        return wf.at[0, pl.ds((b - 8) * BLOCK + row, HALF), :]

    mine = pl.multiple_of(sec * HALF, HALF)
    other = pl.multiple_of((1 - sec) * HALF, HALF)

    def to_stage(b):
        return pltpu.make_async_copy(own_block(b, mine), stage.at[b], in_sem.at[b])

    def to_place(b):
        return pltpu.make_async_copy(
            stage.at[b], full.at[sec * per_layer + b, z, y, x, pl.ds(mine, HALF), :], place_sem.at[b]
        )

    def cross(b):
        return pltpu.make_async_remote_copy(
            src_ref=own_block(b, other),
            dst_ref=full.at[sec * per_layer + b, z, y, x, pl.ds(other, HALF), :],
            send_sem=cross_send.at[b],
            recv_sem=cross_recv.at[b],
            device_id=dev_core,
            device_id_type=MESH,
        )

    take_vec = pltpu.make_async_copy(own_vec, vec.at[sec], vec_sem.at[0])
    give_vec = pltpu.make_async_remote_copy(
        src_ref=own_vec,
        dst_ref=vec.at[sec],
        send_sem=vec_sem.at[1],
        recv_sem=vec_sem.at[2],
        device_id=dev_core,
        device_id_type=MESH,
    )

    def begin():
        for b in range(per_layer):
            to_stage(b).start()
        take_vec.start()
        barrier = pltpu.get_barrier_semaphore()
        for device in (dev_x, dev_y, dev_core):
            pl.semaphore_signal(barrier, inc=1, device_id=device, device_id_type=MESH)

        @pl.when(z < 3)
        def _():
            pl.semaphore_signal(barrier, inc=1, device_id=dev_up, device_id_type=MESH)

        @pl.when(z > 0)
        def _():
            pl.semaphore_signal(barrier, inc=1, device_id=dev_down, device_id_type=MESH)

        pl.semaphore_wait(barrier, 3 + jnp.minimum(z, 1) + jnp.minimum(3 - z, 1))
        for b in range(per_layer):
            cross(b).start()
        for b in range(per_layer):
            to_stage(b).wait()
            to_place(b).start()
        give_vec.start()
        take_vec.wait()
        give_vec.wait_send()
        theirs = vec.at[1 - sec]
        pltpu.make_async_remote_copy(
            src_ref=theirs,
            dst_ref=theirs,
            send_sem=vec_sem.at[1],
            recv_sem=vec_sem.at[2],
            device_id=dev_core,
            device_id_type=MESH,
        ).wait_recv()

    def copy(ref, kind, item, device):
        return pltpu.make_async_remote_copy(
            src_ref=ref,
            dst_ref=ref,
            send_sem=send_sem.at[kind],
            recv_sem=recv_sem.at[kind, item],
            device_id=device,
            device_id_type=MESH,
        )

    def views(core):
        rows = slice(core * HALF, (core + 1) * HALF)
        first, last = slice(0, CUT), slice(CUT, LANES)
        if core == 0:
            pair = lambda i, at: full.at[i, at, :, x, rows, last]
            eight_first = lambda i: full.at[i, :, y, :, rows, first]
            eight_last = lambda i: full.at[i, :, :, x, rows, last]
            towards = (dev_x, dev_y)
        else:
            pair = lambda i, at: full.at[i, at, y, :, rows, last]
            eight_first = lambda i: full.at[i, :, :, x, rows, first]
            eight_last = lambda i: full.at[i, :, y, :, rows, last]
            towards = (dev_y, dev_x)
        return (
            towards,
            lambda i, at: full.at[i, at, y, x, rows, first],
            lambda i: full.at[i, :, y, x, rows, first],
            eight_first,
            lambda i, at: full.at[i, at, y, x, rows, last],
            pair,
            eight_last,
            lambda i: full.at[i, :, :, :, rows, :],
        )

    def z_send(base, block, hop, item, at):
        if at < 3 and at - (hop - 1) >= 0:
            copy(block(item, at - (hop - 1)), base + hop - 1, item, dev_up).start()
        if at > 0 and at + (hop - 1) <= 3:
            copy(block(item, at + (hop - 1)), base + 2 + hop, item, dev_down).start()

    def z_recv(base, block, hop, item, at):
        if at - hop >= 0:
            copy(block(item, at - hop), base + hop - 1, item, dev_up).wait_recv()
        if at + hop <= 3:
            copy(block(item, at + hop), base + 2 + hop, item, dev_down).wait_recv()

    def step_at(t, at, core):
        (dev_u, dev_v), own_a, col_a, eight_a, own_d, pair_d, eight_d, whole = views(core)
        turns = [t - offset for offset in STAGES]

        def live(item):
            return (item >= 0) & (item < items)

        item = turns[0]

        @pl.when(live(item))
        def _():
            layer, b = item // per_layer, item % per_layer

            @pl.when(layer == core)
            def _():
                pltpu.make_async_copy(
                    stage.at[b], full.at[item, z, y, x, pl.ds(core * HALF, HALF), :], place_sem.at[b]
                ).wait()

            @pl.when(layer != core)
            def _():
                mine_there = full.at[item, z, y, x, pl.ds(core * HALF, HALF), :]
                pltpu.make_async_remote_copy(
                    src_ref=mine_there,
                    dst_ref=mine_there,
                    send_sem=cross_send.at[b],
                    recv_sem=cross_recv.at[b],
                    device_id=dev_core,
                    device_id_type=MESH,
                ).wait_recv()

            z_send(0, own_a, 1, item, at)
            copy(own_d(item, at), 8, item, dev_v).start()

        item1 = turns[1]

        @pl.when(live(item1))
        def _():
            z_recv(0, own_a, 1, item1, at)
            z_send(0, own_a, 2, item1, at)
            copy(own_d(item1, at), 8, item1, dev_v).wait_recv()
            z_send(9, pair_d, 1, item1, at)

        item2 = turns[2]

        @pl.when(live(item2))
        def _():
            z_recv(0, own_a, 2, item2, at)
            z_send(0, own_a, 3, item2, at)
            z_recv(9, pair_d, 1, item2, at)
            z_send(9, pair_d, 2, item2, at)

        item3 = turns[3]

        @pl.when(live(item3))
        def _():
            z_recv(0, own_a, 3, item3, at)
            copy(col_a(item3), 6, item3, dev_u).start()
            z_recv(9, pair_d, 2, item3, at)
            z_send(9, pair_d, 3, item3, at)

        item4 = turns[4]

        @pl.when(live(item4))
        def _():
            copy(col_a(item4), 6, item4, dev_u).wait_recv()
            copy(eight_a(item4), 7, item4, dev_v).start()
            z_recv(9, pair_d, 3, item4, at)
            copy(eight_d(item4), 15, item4, dev_u).start()

        item5 = turns[5]

        @pl.when(live(item5))
        def _():
            copy(eight_a(item5), 7, item5, dev_v).wait_recv()
            copy(eight_d(item5), 15, item5, dev_u).wait_recv()
            copy(whole(item5), 16, item5, dev_core).start()

    def step(t):
        for at in range(4):
            for core in range(2):

                @pl.when((z == at) & (sec == core))
                def _():
                    step_at(t, at, core)

    def arrived(item):
        for core in range(2):

            @pl.when(sec == core)
            def _():
                copy(views(1 - core)[-1](item), 16, item, dev_core).wait_recv()

    def end():
        for b in range(per_layer):
            cross(b).wait_send()
        for core in range(2):

            @pl.when(sec == core)
            def _():
                _, own_a, col_a, eight_a, own_d, pair_d, eight_d, whole = views(core)
                every = slice(None)

                def sent(ref, kind):
                    copy(ref, kind, 0, dev_core).wait_send()

                sent(whole(every), 16)
                sent(col_a(every), 6)
                sent(eight_a(every), 7)
                sent(eight_d(every), 15)
                sent(own_d(every, 0), 8)
                for hop in (1, 2, 3):
                    for base, block in ((0, own_a), (9, pair_d)):

                        @pl.when((z < 3) & (z - (hop - 1) >= 0))
                        def _():
                            sent(block(every, 0), base + hop - 1)

                        @pl.when((z > 0) & (z + (hop - 1) <= 3))
                        def _():
                            sent(block(every, 0), base + 2 + hop)

    return begin, step, arrived, end


def wide(ref, columns):
    block = ref[:, :, :, :, columns]
    return block.reshape(-1, block.shape[-1])


def dot_nt(left, right):
    return lax.dot_general(left, right, (((1,), (1,)), ((), ())), preferred_element_type=jnp.float32)


def dot_nn(left, right):
    return jnp.dot(left, right, preferred_element_type=jnp.float32)


def pair_bias(codes):
    down = jnp.broadcast_to(codes, (128, codes.shape[1])).T[:, :1]
    return jnp.where(down == codes, 0.0, -1000000000.0)


def lane_half(pair, half):
    lanes = lax.broadcasted_iota(jnp.int32, pair.shape, 1)
    return jnp.where((lanes < HEAD_DIM) == (half == 0), pair, jnp.zeros_like(pair))


TILE = 256


def forward_kernel(items, with_links, *refs):
    if with_links:
        wq, wo, wi, wf = refs[:4]
        refs = refs[4:]
    else:
        given, given_vec = refs[:2]
        refs = refs[2:]
    if with_links:
        own_vec, refs = refs[0], refs[1:]
    tokens, codes = refs[:2]
    refs = refs[2:]
    if with_links:
        full, refs = refs[0], refs[1:]
    else:
        full = given
    qkv_out, prob_out, ctx_out, slope_out, norm_out, inv_out, y_out, vec_out = refs[:8]
    refs = refs[8:]
    (x, vec, m_qkv, m_attn, m_hidden, m_final, qkv, ctx, hid, act, slope, acc, bias, stage_p, stage_n, stage_i) = refs[:16]
    load_sem, x_sem, vec_sem, p_sem, save_sem = refs[16:21]
    refs = refs[21:]
    sec = lax.axis_index("section")
    per_layer = items // 2

    take_x = pltpu.make_async_copy(tokens.at[sec, 0], x, x_sem.at[0])
    take_x.start()
    if with_links:
        begin_links, step_links, arrived, end_links = link_plan(items, wq, wo, wi, wf, own_vec, full, vec, vec_sem, *refs)
        begin_links()
    else:
        take_vec = pltpu.make_async_copy(given_vec, vec, vec_sem.at[0])
        take_vec.start()
        take_vec.wait()
    bias[...] = pair_bias(codes[sec])
    take_x.wait()
    put_vec = pltpu.make_async_copy(vec, vec_out, x_sem.at[1])
    put_vec.start()

    def load(item):
        b = item % per_layer

        def into(b):
            if b < 3:
                return m_qkv.at[:, :, :, :, b * LANES : (b + 1) * LANES]
            if b == 3:
                return m_attn
            if b < 8:
                return m_hidden.at[:, :, :, :, (b - 4) * LANES : (b - 3) * LANES]
            return m_final.at[(b - 8) // 2, :, :, :, ((b - 8) % 2) * BLOCK : ((b - 8) % 2 + 1) * BLOCK, :]

        for k in range(per_layer):

            @pl.when(b == k)
            def _():
                pltpu.make_async_copy(full.at[item], into(k), load_sem.at[k]).start()

    def loaded(b):
        pltpu.make_async_copy(full.at[0], m_attn, load_sem.at[b]).wait()

    def row(layer, index):
        return vec[layer, index : index + 1, :]

    def project(layer, b):
        scale = jnp.where(b == 0, 0.125, 1.0)
        shift = jnp.where(b == 0, row(layer, 0), jnp.where(b == 2, row(layer, 1), 0.0))
        at = pl.multiple_of(b * LANES, LANES)
        for n in range(0, LANES, TILE):
            columns = pl.ds(at + n, TILE)
            out = dot_nn(x[...], wide(m_qkv, columns)) + shift[:, n : n + TILE]
            qkv[:, columns] = (out.astype(jnp.bfloat16).astype(jnp.float32) * scale).astype(jnp.bfloat16)

    def save_p(layer, p):
        slot = p % 2
        return pltpu.make_async_copy(stage_p.at[slot], prob_out.at[layer, p], p_sem.at[slot])

    def attend(layer, first, last):
        def one(p, _):
            @pl.when(p >= 2)
            def _():
                save_p(layer, p).wait()

            at = pl.multiple_of(p * 128, 128)
            q, k, v = (qkv[:, pl.ds(part * LANES + at, 128)] for part in range(3))
            total = None
            for half in range(2):
                scores = dot_nt(lane_half(q, half), k) + bias[...]
                exps = jnp.exp(scores - jnp.max(scores, -1, keepdims=True))
                probs = (exps / jnp.sum(exps, -1, keepdims=True)).astype(jnp.bfloat16)
                stage_p[p % 2, half] = probs
                out = dot_nn(probs, lane_half(v, half))
                total = out if total is None else total + out
            ctx[:, pl.ds(at, 128)] = total.astype(jnp.bfloat16)
            save_p(layer, p).start()
            return 0

        lax.fori_loop(first, last, one, 0)

    def save(which, layer):
        pairs = (
            (qkv, qkv_out.at[layer]),
            (ctx, ctx_out.at[layer]),
            (slope, slope_out.at[layer]),
            (stage_n, norm_out.at[layer, 0]),
            (stage_i, inv_out.at[layer, 0]),
            (stage_n, norm_out.at[layer, 1]),
            (stage_i, inv_out.at[layer, 1]),
            (x, y_out.at[layer]),
        )
        return pltpu.make_async_copy(*pairs[which], save_sem.at[which])

    def normalize(layer, which, put):
        for r in range(0, SEQ, 128):
            rows = slice(r, r + 128)
            residual = acc[rows, :]
            centered = residual - jnp.mean(residual, -1, keepdims=True)
            inverse = lax.rsqrt(jnp.mean(centered * centered, -1, keepdims=True) + epsilon)
            normed = centered * inverse
            stage_n[rows, :] = normed.astype(jnp.bfloat16)
            stage_i[rows, :] = jnp.broadcast_to(inverse, (128, 128))
            put[rows, :] = (normed * row(layer, 8 + which) + row(layer, 10 + which)).astype(jnp.bfloat16)

    def attn_out(layer):
        for n in range(0, LANES, TILE):
            columns = slice(n, n + TILE)
            acc[:, columns] = x[:, columns].astype(jnp.float32) + (
                dot_nn(ctx[...], wide(m_attn, columns)) + row(layer, 2)[:, columns]
            )
        normalize(layer, 0, hid)

    def ffn_in(layer, j):
        shift = vec[layer, pl.ds(3 + j, 1), :]
        at = pl.multiple_of(j * LANES, LANES)
        for n in range(0, LANES, TILE):
            pre = dot_nn(hid[...], wide(m_hidden, pl.ds(at + n, TILE))) + shift[:, n : n + TILE]
            cdf = 0.5 * (1.0 + lax.erf(pre * math.sqrt(0.5)))
            pdf = jnp.exp(pre * pre * -0.5) * (1.0 / math.sqrt(2.0 * math.pi))
            value = (pre * cdf).astype(jnp.bfloat16)
            grade = (cdf + pre * pdf).astype(jnp.bfloat16)
            to = pl.ds(pl.multiple_of(j * 512 + n // 2, 128), 128)
            for half in range(2):
                act[half, :, to] = value[:, half * 128 : (half + 1) * 128]
                slope[half, :, to] = grade[:, half * 128 : (half + 1) * 128]

    def ffn_out(layer, half):
        for n in range(0, LANES, TILE):
            columns = slice(n, n + TILE)
            out = dot_nn(act[half], wide(m_final.at[half], columns))
            if half == 0:
                acc[:, columns] = hid[:, columns].astype(jnp.float32) + (out + row(layer, 7)[:, columns])
            else:
                acc[:, columns] += out

    def compute(c):
        layer, b = c // per_layer, c % per_layer

        @pl.when((b == 0) & (layer == 1))
        def _():
            save(7, 0).wait()

        @pl.when(b <= 2)
        def _():
            loaded(b)
            project(layer, b)

        @pl.when(b == 2)
        def _():
            save(0, layer).start()
            attend(layer, 0, 2)

        @pl.when(b == 3)
        def _():
            loaded(3)
            attend(layer, 2, 5)

        @pl.when(b == 4)
        def _():
            loaded(4)
            attend(layer, 5, 8)

        @pl.when(b == 5)
        def _():
            save(1, layer).start()
            loaded(5)
            attn_out(layer)
            save(3, layer).start()
            save(4, layer).start()

        @pl.when((b >= 5) & (b <= 8))
        def _():
            ffn_in(layer, b - 5)

        @pl.when(b == 6)
        def _():
            loaded(6)
            save_p(layer, 0).wait()
            save_p(layer, 1).wait()
            save(0, layer).wait()
            save(1, layer).wait()

        @pl.when(b == 7)
        def _():
            loaded(7)

        @pl.when(b == 8)
        def _():
            save(2, layer).start()
            loaded(8)

        @pl.when(b == 9)
        def _():
            loaded(9)
            ffn_out(layer, 0)
            save(3, layer).wait()
            save(4, layer).wait()

        @pl.when(b == 10)
        def _():
            loaded(10)
            save(2, layer).wait()

        @pl.when(b == 11)
        def _():
            loaded(11)
            ffn_out(layer, 1)
            normalize(layer, 1, x)
            save(5, layer).start()
            save(6, layer).start()
            save(7, layer).start()
            save(5, layer).wait()
            save(6, layer).wait()

    def step(t, _):
        if with_links:
            step_links(t)
        first = t - LOAD

        @pl.when((first >= 0) & (first < items))
        def _():
            if with_links:
                arrived(first)
            load(first)

        second = t - LOAD - 1

        @pl.when((second >= 0) & (second < items))
        def _():
            compute(second)

        return 0

    lax.fori_loop(0, items + LOAD + 1, step, 0)
    save(7, 1).wait()
    put_vec.wait()
    if with_links:
        end_links()


def forward(tokens, codes, vec, weights):
    items = 24
    with_links = len(weights) == 4
    low, wide_type = jnp.bfloat16, jnp.float32
    in_hbm = pl.BlockSpec(memory_space=pltpu.HBM)
    in_vmem = pl.BlockSpec(memory_space=pltpu.VMEM)
    shape = jax.ShapeDtypeStruct
    full = shape((items, 4, 2, 2, BLOCK, LANES), low)
    saved = (
        shape((2, SEQ, 3 * LANES), low),
        shape((2, 8, 2, SEQ, SEQ), low),
        shape((2, SEQ, LANES), low),
        shape((2, 2, SEQ, 2 * LANES), low),
        shape((2, 2, SEQ, LANES), low),
        shape((2, 2, SEQ, 128), wide_type),
        shape((2, SEQ, LANES), low),
        shape((2, 16, LANES), wide_type),
    )
    scratch = [
        pltpu.VMEM((SEQ, LANES), low),
        pltpu.VMEM((2, 16, LANES), wide_type),
        pltpu.VMEM((4, 2, 2, BLOCK, 3 * LANES), low),
        pltpu.VMEM((4, 2, 2, BLOCK, LANES), low),
        pltpu.VMEM((4, 2, 2, BLOCK, 4 * LANES), low),
        pltpu.VMEM((2, 4, 2, 2, 2 * BLOCK, LANES), low),
        pltpu.VMEM((SEQ, 3 * LANES), low),
        pltpu.VMEM((SEQ, LANES), low),
        pltpu.VMEM((SEQ, LANES), low),
        pltpu.VMEM((2, SEQ, 2 * LANES), low),
        pltpu.VMEM((2, SEQ, 2 * LANES), low),
        pltpu.VMEM((SEQ, LANES), wide_type),
        pltpu.VMEM((SEQ, SEQ), wide_type),
        pltpu.VMEM((2, 2, SEQ, SEQ), low),
        pltpu.VMEM((SEQ, LANES), low),
        pltpu.VMEM((SEQ, 128), wide_type),
        pltpu.SemaphoreType.DMA((12,)),
        pltpu.SemaphoreType.DMA((2,)),
        pltpu.SemaphoreType.DMA((3,)),
        pltpu.SemaphoreType.DMA((2,)),
        pltpu.SemaphoreType.DMA((8,)),
    ]
    if with_links:
        operands = (*weights, vec, tokens, codes)
        specs = [in_hbm] * 6 + [in_vmem]
        outs = (full, *saved)
        scratch += [
            pltpu.VMEM((items // 2, HALF, LANES), low),
            pltpu.SemaphoreType.DMA((items // 2,)),
            pltpu.SemaphoreType.DMA((items // 2,)),
            pltpu.SemaphoreType.DMA((items // 2,)),
            pltpu.SemaphoreType.DMA((items // 2,)),
            pltpu.SemaphoreType.DMA((17,)),
            pltpu.SemaphoreType.DMA((17, items)),
        ]
        params = pltpu.CompilerParams(collective_id=0, has_side_effects=True, vmem_limit_bytes=VMEM_LIMIT)
    else:
        operands = (weights[0], vec, tokens, codes)
        specs = [in_hbm] * 3 + [in_vmem]
        outs = saved
        params = pltpu.CompilerParams(vmem_limit_bytes=VMEM_LIMIT)
    results = pl.pallas_call(
        partial(forward_kernel, items, with_links),
        out_shape=outs,
        in_specs=specs,
        out_specs=tuple([in_hbm] * len(outs)),
        scratch_shapes=scratch,
        compiler_params=params,
    )(*operands)
    return results if with_links else (weights[0], *results)


def backward_kernel(
    cotangent,
    full,
    vec_in,
    qkv_in,
    prob_in,
    ctx_in,
    slope_in,
    norm_in,
    inv_in,
    grad_out,
    sums,
    vec,
    m_qkv,
    m_attn,
    m_hidden,
    m_final,
    qkv,
    ctx,
    slope,
    norms,
    invs,
    probs,
    grad,
    rounded_grad,
    pre_grad,
    proj_grad,
    acc,
    sem,
    m_sem,
    p_sem,
    out_sem,
):
    sec = lax.axis_index("section")

    def start(copies):
        for copy in copies:
            copy.start()

    def wait(copies):
        for copy in copies:
            copy.wait()

    def fetch_final(layer, half):
        return [
            pltpu.make_async_copy(
                full.at[layer * 12 + 8 + 2 * half + g],
                m_final.at[half, :, :, :, g * BLOCK : (g + 1) * BLOCK, :],
                m_sem.at[2 * half + g],
            )
            for g in range(2)
        ]

    def fetch_hidden(layer):
        return [
            pltpu.make_async_copy(
                full.at[layer * 12 + 4 + j], m_hidden.at[:, :, :, :, j * LANES : (j + 1) * LANES], m_sem.at[4 + j]
            )
            for j in range(4)
        ]

    def fetch_attn(layer):
        return [pltpu.make_async_copy(full.at[layer * 12 + 3], m_attn, m_sem.at[8])]

    def fetch_qkv(layer):
        return [
            pltpu.make_async_copy(
                full.at[layer * 12 + j], m_qkv.at[:, :, :, :, j * LANES : (j + 1) * LANES], m_sem.at[9 + j]
            )
            for j in range(3)
        ]

    def fetch_norm(layer, which):
        return [
            pltpu.make_async_copy(norm_in.at[layer, which], norms.at[which], sem.at[2 * which]),
            pltpu.make_async_copy(inv_in.at[layer, which], invs.at[which], sem.at[2 * which + 1]),
        ]

    def fetch_slope(layer, half):
        return [pltpu.make_async_copy(slope_in.at[layer, half], slope.at[half], sem.at[4 + half])]

    def fetch_heads(layer):
        return [
            pltpu.make_async_copy(qkv_in.at[layer], qkv, sem.at[6]),
            pltpu.make_async_copy(ctx_in.at[layer], ctx, sem.at[7]),
        ]

    def fetch_probs(layer, p):
        return [pltpu.make_async_copy(prob_in.at[layer, p], probs.at[p % 2], p_sem.at[p % 2])]

    take_grad = pltpu.make_async_copy(cotangent.at[sec, 0], grad, sem.at[8])
    take_vec = pltpu.make_async_copy(vec_in, vec, sem.at[9])
    take_grad.start()
    start(fetch_norm(1, 1))
    take_vec.start()
    start(fetch_final(1, 0) + fetch_slope(1, 0) + fetch_final(1, 1) + fetch_slope(1, 1) + fetch_hidden(1))
    start(fetch_norm(1, 0) + fetch_attn(1) + fetch_heads(1))
    start(fetch_probs(1, 0) + fetch_probs(1, 1) + fetch_qkv(1))
    take_grad.wait()
    take_vec.wait()

    def put_grad(layer):
        return pltpu.make_async_copy(grad, grad_out.at[layer], out_sem.at[0])

    def column_sum(values):
        return jnp.sum(values.astype(jnp.float32), 0, keepdims=True)

    def norm_back(layer, which, upstream_of):
        gain = vec[layer, 8 + which : 9 + which, :]
        total = jnp.zeros((1, LANES), jnp.float32)
        for r in range(0, SEQ, 128):
            rows = slice(r, r + 128)
            upstream = upstream_of(rows) * gain
            normed = norms[which, rows, :].astype(jnp.float32)
            back = invs[which, rows, 0:1] * (
                upstream
                - jnp.mean(upstream, -1, keepdims=True)
                - normed * jnp.mean(upstream * normed, -1, keepdims=True)
            )
            acc[rows, :] = back
            low = back.astype(jnp.bfloat16)
            rounded_grad[rows, :] = low
            total = total + column_sum(low)
        return total

    def one_layer(s, _):
        layer = 1 - s

        def prefetch(copies):
            @pl.when(s == 0)
            def _():
                start(copies)

        wait(fetch_norm(layer, 1))
        sums[layer, 7:8, :] = norm_back(layer, 1, lambda rows: grad[rows, :].astype(jnp.float32))
        prefetch(fetch_norm(0, 1))
        for half in range(2):
            wait(fetch_final(layer, half) + fetch_slope(layer, half))
            for n in range(0, 2048, TILE):
                chip = n // 128
                block = m_final[half, chip // 4, (chip // 2) % 2].reshape(TILE, LANES)
                back = dot_nt(rounded_grad[...], block) * slope[half, :, n : n + TILE].astype(jnp.float32)
                low = back.astype(jnp.bfloat16)
                total = column_sum(low)
                for k in range(2):
                    at = (chip + k) * 256 + half * 128
                    part = slice(k * 128, (k + 1) * 128)
                    pre_grad[:, at : at + 128] = low[:, part]
                    sums[layer, 3 + at // LANES : 4 + at // LANES, at % LANES : at % LANES + 128] = total[:, part]
            prefetch(fetch_final(0, half) + fetch_slope(0, half))
        wait(fetch_hidden(layer))
        for n in range(0, LANES, TILE):
            block = m_hidden[n // TILE].reshape(TILE, 4 * LANES)
            acc[:, n : n + TILE] += dot_nt(pre_grad[...], block)
        prefetch(fetch_hidden(0))
        wait(fetch_norm(layer, 0))
        sums[layer, 2:3, :] = norm_back(
            layer, 0, lambda rows: acc[rows, :].astype(jnp.bfloat16).astype(jnp.float32)
        )
        prefetch(fetch_norm(0, 0))

        @pl.when(s == 1)
        def _():
            put_grad(1).wait()

        wait(fetch_attn(layer))
        for n in range(0, LANES, TILE):
            block = m_attn[n // TILE].reshape(TILE, LANES)
            grad[:, n : n + TILE] = dot_nt(rounded_grad[...], block).astype(jnp.bfloat16)
        prefetch(fetch_attn(0))
        wait(fetch_heads(layer))

        def one_pair(p, _):
            wait(fetch_probs(layer, p))
            at = pl.multiple_of(p * 128, 128)
            q, k, v = (qkv[:, pl.ds(part * LANES + at, 128)] for part in range(3))
            upper = grad[:, pl.ds(at, 128)]
            product = upper.astype(jnp.float32) * ctx[:, pl.ds(at, 128)].astype(jnp.float32)
            q_t, upper_t = q.T, upper.T
            grad_q = None
            grad_k, grad_v = [], []
            for half in range(2):
                weights = probs[p % 2, half]
                delta = jnp.sum(lane_half(product, half), -1, keepdims=True)
                scores = dot_nt(lane_half(upper, half), v)
                low = (weights.astype(jnp.float32) * (scores - delta)).astype(jnp.bfloat16)
                part = dot_nn(low, lane_half(k, half))
                grad_q = part if grad_q is None else grad_q + part
                here = slice(half * HEAD_DIM, (half + 1) * HEAD_DIM)
                grad_k.append(dot_nn(q_t[here], low))
                grad_v.append(dot_nn(upper_t[here], weights))
            back_q = (grad_q * 0.125).astype(jnp.bfloat16)
            back_v = jnp.concatenate(grad_v, 0).astype(jnp.bfloat16).T
            proj_grad[:, pl.ds(at, 128)] = back_q
            proj_grad[:, pl.ds(LANES + at, 128)] = jnp.concatenate(grad_k, 0).astype(jnp.bfloat16).T
            proj_grad[:, pl.ds(2 * LANES + at, 128)] = back_v
            sums[layer, 0:1, pl.ds(at, 128)] = column_sum(back_q)
            sums[layer, 1:2, pl.ds(at, 128)] = column_sum(back_v)

            @pl.when(p < 6)
            def _():
                start(fetch_probs(layer, p + 2))

            return 0

        lax.fori_loop(0, 8, one_pair, 0)
        prefetch(fetch_heads(0) + fetch_probs(0, 0) + fetch_probs(0, 1))
        wait(fetch_qkv(layer))
        for n in range(0, LANES, TILE):
            block = m_qkv[n // TILE].reshape(TILE, 3 * LANES)
            columns = slice(n, n + TILE)
            grad[:, columns] = (acc[:, columns] + dot_nt(proj_grad[...], block)).astype(jnp.bfloat16)
        prefetch(fetch_qkv(0))
        put_grad(layer).start()
        return 0

    lax.fori_loop(0, 2, one_layer, 0)
    put_grad(0).wait()


def backward(cotangent, full, vec, saved):
    qkv, probs, ctx, slope, norms, invs = saved
    in_hbm = pl.BlockSpec(memory_space=pltpu.HBM)
    in_vmem = pl.BlockSpec(memory_space=pltpu.VMEM)
    low, wide_type = jnp.bfloat16, jnp.float32
    return pl.pallas_call(
        backward_kernel,
        out_shape=(
            jax.ShapeDtypeStruct((2, SEQ, LANES), low),
            jax.ShapeDtypeStruct((2, 8, LANES), wide_type),
        ),
        in_specs=[in_hbm] * 9,
        out_specs=(in_hbm, in_vmem),
        scratch_shapes=[
            pltpu.VMEM((2, 16, LANES), wide_type),
            pltpu.VMEM((4, 2, 2, BLOCK, 3 * LANES), low),
            pltpu.VMEM((4, 2, 2, BLOCK, LANES), low),
            pltpu.VMEM((4, 2, 2, BLOCK, 4 * LANES), low),
            pltpu.VMEM((2, 4, 2, 2, 2 * BLOCK, LANES), low),
            pltpu.VMEM((SEQ, 3 * LANES), low),
            pltpu.VMEM((SEQ, LANES), low),
            pltpu.VMEM((2, SEQ, 2 * LANES), low),
            pltpu.VMEM((2, SEQ, LANES), low),
            pltpu.VMEM((2, SEQ, 128), wide_type),
            pltpu.VMEM((2, 2, SEQ, SEQ), low),
            pltpu.VMEM((SEQ, LANES), low),
            pltpu.VMEM((SEQ, LANES), low),
            pltpu.VMEM((SEQ, 4 * LANES), low),
            pltpu.VMEM((SEQ, 3 * LANES), low),
            pltpu.VMEM((SEQ, LANES), wide_type),
            pltpu.SemaphoreType.DMA((10,)),
            pltpu.SemaphoreType.DMA((12,)),
            pltpu.SemaphoreType.DMA((2,)),
            pltpu.SemaphoreType.DMA((1,)),
        ],
        compiler_params=pltpu.CompilerParams(vmem_limit_bytes=VMEM_LIMIT),
    )(cotangent, full, vec, qkv, probs, ctx, slope, norms, invs)


def gather(w_qkv, w_out, w_in, w_ffn_out):
    matrices = [lax.all_gather(w[0], "dp", axis=0, tiled=True) for w in (w_qkv, w_out, w_in, w_ffn_out)]
    qkv, attn, hidden, final = matrices
    blocks = [qkv[:, b * LANES : (b + 1) * LANES] for b in range(3)] + [attn]
    blocks += [hidden[:, b * LANES : (b + 1) * LANES] for b in range(4)]
    final = final.reshape(16, 4, BLOCK, LANES).transpose(1, 0, 2, 3).reshape(4, 1024, LANES)
    own = jnp.concatenate([jnp.stack(blocks), final])
    return lax.all_gather(own, "section", axis=0, tiled=True).reshape(24, 4, 2, 2, BLOCK, LANES)


def on_device(
    tokens,
    segment_ids,
    row_lengths,
    w_qkv,
    w_out,
    w_in,
    w_ffn_out,
    bias_q,
    bias_v,
    bias_out,
    bias_in,
    bias_ffn_out,
    ln_gain,
    ln_shift,
    out_cotangent,
):
    sec = lax.axis_index("section")
    weights = (w_qkv, w_out, w_in, w_ffn_out)
    vec = jnp.concatenate(
        [bias_q, bias_v, bias_out, bias_in.reshape(4, LANES), bias_ffn_out, ln_gain[0], ln_shift[0], jnp.zeros((4, LANES))]
    )
    if w_qkv.shape[1] != BLOCK:
        weights = (gather(*weights),)
        vec = lax.all_gather(vec, "section", axis=0)
    valid = jnp.arange(SEQ, dtype=jnp.int32) < row_lengths[:, :, None]
    codes = segment_ids * 2 + valid.astype(jnp.int32)
    full, *saved, tops, vec = forward(tokens, codes, vec, weights)
    grads, sums = backward(out_cotangent, full, vec, saved)

    def swap(array):
        return lax.ppermute(array, "section", [(0, 1), (1, 0)])

    def placed(both):
        got = swap(jnp.where(sec == 0, both[1], both[0]))
        placed = jnp.where(sec == 0, jnp.stack([both[0], got]), jnp.stack([got, both[1]]))
        return placed[None, :, None]

    sums = jnp.where(sec == 0, sums[0], sums[1]) + swap(jnp.where(sec == 0, sums[1], sums[0]))
    sums = lax.psum(sums, "dp")
    totals = (sums[0:1], sums[1:2], sums[2:3], sums[3:7].reshape(1, 4 * LANES), sums[7:8])
    return (placed(tops), placed(grads)) + totals


def solution(mesh):
    placed = (
        P(None, "dp", None, None),
        P(None, "dp", None),
        P(None, "dp"),
        P("section", "dp", None),
        P("section", "dp", None),
        P("section", "dp", None),
        P("section", "dp", None),
        P("section", None),
        P("section", None),
        P("section", None),
        P("section", None),
        P("section", None),
        P("section", None, None),
        P("section", None, None),
        P(None, "dp", None, None),
    )
    return jax.shard_map(
        on_device,
        mesh=mesh,
        in_specs=placed,
        out_specs=(
            P("section", None, "dp", None, None),
            P("section", None, "dp", None, None),
            P("section", None),
            P("section", None),
            P("section", None),
            P("section", None),
            P("section", None),
        ),
        check_vma=False,
    )
```

time: 3310 us -> 367 us (0.11)
  waiting for transfers between devices: 2430 us -> 2.13 us
  matrix products: 349 us -> 0 us
  Pallas kernels: 0 us -> 270 us
  blocking collectives: 222 us -> 74.8 us
  starting transfers between devices: 78.1 us -> 0.99 us
  local copies, waits for them, and re-layouts: 79.8 us -> 4.51 us
  other arithmetic: 82.4 us -> 13.7 us
    all_gather x24 -> x0, waiting for transfers between devices: 2340 us -> none  [the longest x3 342 us: forward_step(): lax.all_gather(w_ffn_out, 'dp', axis=1, tiled=True)]
    dot_general x36 -> x0, matrix products: 327 us -> none  [the longest x4 81.8 us: layer_forward(): jnp.dot(activated, mat_final, preferred_element_type=jnp.float32)]
    pallas_call x0 -> x2, Pallas kernels: none -> 270 us  [the longest x1 207 us: forward(): pl.pallas_call(partial(forward_kernel, items, with_links), out_shape=outs...]
    psum x3 -> x1, blocking collectives: 222 us -> 74.8 us  [on_device(): sums = lax.psum(sums, 'dp')]
    ppermute x6 -> x3, waiting for transfers between devices: 78.5 us -> 2.13 us  [swap(): return lax.ppermute(array, 'section', [(0, 1), (1, 0)])]
    ppermute x6 -> x3, starting transfers between devices: 77.3 us -> 0.99 us  [swap(): return lax.ppermute(array, 'section', [(0, 1), (1, 0)])]
  transfers between devices with their start and end apart: 30 -> 3, of which waited for: 28 -> 1; matrix products, arithmetic and copies ran while one was open for 1% -> 2% of each run, Pallas kernels for 0% -> 0%
where the time goes in v1:
time: 367 us; the launch traced here: 366 us
  Pallas kernels  270 us (74%)
  blocking collectives  74.8 us (20%)
  other arithmetic  13.7 us (4%)
  local copies, waits for them, and re-layouts  4.51 us (1%)
    pallas_call x1, Pallas kernels, forward(): pl.pallas_call(partial(forward_kernel, items, with_links), out_shape=outs...  207 us
    psum x1, blocking collectives, on_device(): sums = lax.psum(sums, 'dp')  74.8 us
    pallas_call x1, Pallas kernels, backward(): pl.pallas_call(backward_kernel, out_shape=(jax.ShapeDtypeStruct((2, SEQ,...  62.3 us
  transfers between devices with their start and end apart: 3, of which 1 were waited for; matrix products, arithmetic and copies ran while one was open for 2% of the time, Pallas kernels for 0%

profile of v1, /device:TPU:0, one launch (start us, length us, event | category | flops | bytes accessed | tf_op | source)
XLA Modules:
  0.0 366.4 jit_solution(4738845708375599985)
XLA Ops:
  0.6 0.5 broadcast.48
  1.1 1.4 reduce.3
  2.6 1.4 fusion.refs_6_
  3.9 2.7 concatenate.31.refs_4_
  6.7 207.2 %shard_map.201 = (bf16[24,4,2,2,64,1024]{5,4,3,2,1,0:T(8,128)(2,1)}, bf16[2,512,3072]{2,1,0:T(8,128)(2,1)}, bf16[2,8,2,512,512]{4,3,2,1,0:T(8,128)(2,1)}, bf16[2...) custom-call(bf16[1,64,3072]{2,1,0:T(8,128)(2,1)} %refs_0_.1, ...), custom_call_target="tpu_custom_call" | custom-call | tf_op jit(solution)/shard_map/pallas_call | solution.py:630
  213.9 62.3 %shard_map.202 = (bf16[2,512,1024]{2,1,0:T(8,128)(2,1)}, f32[2,8,1024]{2,1,0:T(8,128)}) custom-call(bf16[2,1,512,1024]{3,2,1,0:T(8,128)(2,1)} %cotangent.1, bf16[24,4,2,2,64,1024]{5,4,3,2,1,0:T(8,128)(2,1)} %get-tuple-element.19.full, f32[2,16,1024]{2,1,0:T(8,128)} %get-tuple-element.20.vec_in, bf16[2,512,3072]{2,1,0:T(8,128)(2,1)} %get-tuple-element.21.qkv_in, ...), custom_call_target="tpu_custom_call" | custom-call | tf_op jit(solution)/shard_map/pallas_call | solution.py:866
  276.2 0.0 copy-start.1
  276.2 2.9 slice_bitcast_fusion
  279.1 0.4 collective-permute-start.1
  279.5 0.0 copy-done.1
  279.5 0.0 copy-start.2
  279.5 1.5 slice_bitcast_fusion.2
  281.0 0.1 collective-permute-start
  281.1 0.0 copy-done.2
  281.1 0.5 collective-permute-start.2
  281.6 2.1 collective-permute-done.2
  283.7 74.8 %psum.7 = f32[8,1024]{1,0:T(8,128)S(1)} all-reduce(f32[8,1024]{1,0:T(8,128)S(1)} %bitcast_add_fusion), channel_id=1, replica_groups=mesh['section'=2,'dp'=16] {'dp'}, use_global_device_ids=true, to_apply=%region_0.1 | all-reduce | flops 8192 | bytes 65536 | tf_op jit(solution)/shard_map/psum | solution.py:949
  358.6 0.6 copy.22
  359.2 0.6 fusion.1
  359.8 0.0 collective-permute-done.1
  359.8 3.4 maximum_select_fusion.1
  363.2 0.0 collective-permute-done
  363.2 0.0 copy-done
  363.2 3.2 maximum_select_fusion
  (6 shorter events, 0.0 us)
Async XLA Ops:
  276.2 3.3 copy-start.1
  279.1 80.7 %collective-permute-start.1 = (bf16[512,1024]{1,0:T(8,128)(2,1)}, bf16[512,1024]{1,0:T(8,128)(2,1)}, u32[]{:S(2)}, u32[]{:S(2)}) collective-permute-start(bf16[512,1024]{1,0:T(8,128)(2,1)} %get-tuple-element.30), channel_id=1, source_target_pairs={{0,16},{16,0},{1,17},{17,1},{2,18},{18,2},{3,19},{19,3},{4,20},{20... | collective-permute-start | bytes 3145736 | tf_op jit(solution)/shard_map/ppermute | solution.py:941
  279.5 1.6 copy-start.2
  281.0 82.1 %collective-permute-start = (bf16[512,1024]{1,0:T(8,128)(2,1)}, bf16[512,1024]{1,0:T(8,128)(2,1)}, u32[]{:S(2)}, u32[]{:S(2)}) collective-permute-start(bf16[512,1024]{1,0:T(8,128)(2,1)} %get-tuple-element.33), channel_id=1, source_target_pairs={{0,16},{16,0},{1,17},{17,1},{2,18},{18,2},{3,19},{19,3},{4,20},{20... | collective-permute-start | bytes 3145736 | tf_op jit(solution)/shard_map/ppermute | solution.py:941
  281.1 2.6 collective-permute-start.2
  359.8 3.4 copy-start

commit v2 on v1

v2 whole, which is shorter than its diff:
```python
from functools import partial
import math

import jax
import jax.numpy as jnp
from jax import lax
from jax.experimental import pallas as pl
from jax.experimental.pallas import tpu as pltpu
from jax.sharding import PartitionSpec as P

HEAD_DIM = 64
SEQ = 512
PAIRS = 8
epsilon = 1e-06
VMEM_LIMIT = 60 * 2**20
MESH = pl.DeviceIdType.MESH
ITEMS = 24
PER_LAYER = ITEMS // 2
LANES = 1024
BLOCK = 64
HALF = BLOCK // 2
CUT = 384
STAGES = (1, 2, 3, 4, 6)
LOAD = 7
FRONT = 2
TILE = 256


def link_plan(wq, wo, wi, wf, full, vec, stage, in_sem, place_sem, cross_send, cross_recv, send_sem, recv_sem, vec_sem):
    sec = lax.axis_index("section")
    chip = lax.axis_index("dp")
    per_layer, items = PER_LAYER, ITEMS
    z = chip // 4
    y = (chip // 2) % 2
    x = chip % 2
    dev_x = (sec, z * 4 + y * 2 + 1 - x)
    dev_y = (sec, z * 4 + (1 - y) * 2 + x)
    dev_xy = (sec, z * 4 + (1 - y) * 2 + 1 - x)
    dev_up = (sec, jnp.minimum(z + 1, 3) * 4 + y * 2 + x)
    dev_down = (sec, jnp.maximum(z - 1, 0) * 4 + y * 2 + x)
    dev_core = (1 - sec, chip)
    in_plane = (dev_x, dev_y, dev_xy)
    along_z = tuple((sec, ((z + k) % 4) * 4 + y * 2 + x) for k in (1, 2, 3))

    def own_block(b, row):
        if b < 3:
            return wq.at[0, pl.ds(row, HALF), b * LANES : (b + 1) * LANES]
        if b == 3:
            return wo.at[0, pl.ds(row, HALF), :]
        if b < 8:
            return wi.at[0, pl.ds(row, HALF), (b - 4) * LANES : (b - 3) * LANES]
        return wf.at[0, pl.ds((b - 8) * BLOCK + row, HALF), :]

    mine = pl.multiple_of(sec * HALF, HALF)
    other = pl.multiple_of((1 - sec) * HALF, HALF)

    def to_stage(b):
        return pltpu.make_async_copy(own_block(b, mine), stage.at[b], in_sem.at[b])

    def to_place(b):
        return pltpu.make_async_copy(
            stage.at[b], full.at[sec * per_layer + b, z, y, x, pl.ds(mine, HALF), :], place_sem.at[b]
        )

    def cross(b):
        return pltpu.make_async_remote_copy(
            src_ref=own_block(b, other),
            dst_ref=full.at[sec * per_layer + b, z, y, x, pl.ds(other, HALF), :],
            send_sem=cross_send.at[b],
            recv_sem=cross_recv.at[b],
            device_id=dev_core,
            device_id_type=MESH,
        )

    def give_vec(where):
        return pltpu.make_async_remote_copy(
            src_ref=where,
            dst_ref=where,
            send_sem=vec_sem.at[0],
            recv_sem=vec_sem.at[1],
            device_id=dev_core,
            device_id_type=MESH,
        )

    def begin():
        for b in range(per_layer):
            to_stage(b).start()
        barrier = pltpu.get_barrier_semaphore()
        for device in (dev_core, *in_plane, *along_z):
            pl.semaphore_signal(barrier, inc=1, device_id=device, device_id_type=MESH)
        pl.semaphore_wait(barrier, 7)
        for b in range(per_layer):
            cross(b).start()
        give_vec(vec.at[sec]).start()
        for b in range(per_layer):
            to_stage(b).wait()
            to_place(b).start()

    def vec_here():
        give_vec(vec.at[sec]).wait_send()
        give_vec(vec.at[1 - sec]).wait_recv()

    def copy(ref, kind, item, device):
        return pltpu.make_async_remote_copy(
            src_ref=ref,
            dst_ref=ref,
            send_sem=send_sem.at[kind],
            recv_sem=recv_sem.at[kind, item],
            device_id=device,
            device_id_type=MESH,
        )

    def views(core):
        rows = slice(core * HALF, (core + 1) * HALF)
        first, last = slice(0, CUT), slice(CUT, LANES)
        if core == 0:
            pair = lambda i, at: full.at[i, at, :, x, rows, last]
            eight_first = lambda i: full.at[i, :, y, :, rows, first]
            eight_last = lambda i: full.at[i, :, :, x, rows, last]
            towards = (dev_x, dev_y)
        else:
            pair = lambda i, at: full.at[i, at, y, :, rows, last]
            eight_first = lambda i: full.at[i, :, :, x, rows, first]
            eight_last = lambda i: full.at[i, :, y, :, rows, last]
            towards = (dev_y, dev_x)
        return (
            towards,
            lambda i, at: full.at[i, at, y, x, rows, first],
            lambda i: full.at[i, :, y, x, rows, first],
            eight_first,
            lambda i, at: full.at[i, at, y, x, rows, last],
            pair,
            eight_last,
            lambda i: full.at[i, :, :, :, rows, :],
        )

    def z_send(base, block, hop, item, at):
        if at < 3 and at - (hop - 1) >= 0:
            copy(block(item, at - (hop - 1)), base + hop - 1, item, dev_up).start()
        if at > 0 and at + (hop - 1) <= 3:
            copy(block(item, at + (hop - 1)), base + 2 + hop, item, dev_down).start()

    def z_recv(base, block, hop, item, at):
        if at - hop >= 0:
            copy(block(item, at - hop), base + hop - 1, item, dev_up).wait_recv()
        if at + hop <= 3:
            copy(block(item, at + hop), base + 2 + hop, item, dev_down).wait_recv()

    def step_at(t, at, core):
        (dev_u, dev_v), own_a, col_a, eight_a, own_d, pair_d, eight_d, whole = views(core)
        turns = [t - offset for offset in STAGES]

        def live(item):
            return (item >= 0) & (item < items)

        def first_move(item):
            @pl.when(live(item))
            def _():
                layer, b = item // per_layer, item % per_layer

                @pl.when(layer == core)
                def _():
                    pltpu.make_async_copy(
                        stage.at[b], full.at[item, z, y, x, pl.ds(core * HALF, HALF), :], place_sem.at[b]
                    ).wait()

                @pl.when(layer != core)
                def _():
                    mine_there = full.at[item, z, y, x, pl.ds(core * HALF, HALF), :]
                    pltpu.make_async_remote_copy(
                        src_ref=mine_there,
                        dst_ref=mine_there,
                        send_sem=cross_send.at[b],
                        recv_sem=cross_recv.at[b],
                        device_id=dev_core,
                        device_id_type=MESH,
                    ).wait_recv()

                z_send(0, own_a, 1, item, at)
                copy(own_d(item, at), 8, item, dev_v).start()

        for lead in range(FRONT):
            first_move(t * FRONT + lead)

        item1 = turns[0]

        @pl.when(live(item1))
        def _():
            z_recv(0, own_a, 1, item1, at)
            z_send(0, own_a, 2, item1, at)
            copy(own_d(item1, at), 8, item1, dev_v).wait_recv()
            z_send(9, pair_d, 1, item1, at)

        item2 = turns[1]

        @pl.when(live(item2))
        def _():
            z_recv(0, own_a, 2, item2, at)
            z_send(0, own_a, 3, item2, at)
            z_recv(9, pair_d, 1, item2, at)
            z_send(9, pair_d, 2, item2, at)

        item3 = turns[2]

        @pl.when(live(item3))
        def _():
            z_recv(0, own_a, 3, item3, at)
            copy(col_a(item3), 6, item3, dev_u).start()
            z_recv(9, pair_d, 2, item3, at)
            z_send(9, pair_d, 3, item3, at)

        item4 = turns[3]

        @pl.when(live(item4))
        def _():
            copy(col_a(item4), 6, item4, dev_u).wait_recv()
            copy(eight_a(item4), 7, item4, dev_v).start()
            z_recv(9, pair_d, 3, item4, at)
            copy(eight_d(item4), 15, item4, dev_u).start()

        item5 = turns[4]

        @pl.when(live(item5))
        def _():
            copy(eight_a(item5), 7, item5, dev_v).wait_recv()
            copy(eight_d(item5), 15, item5, dev_u).wait_recv()
            copy(whole(item5), 16, item5, dev_core).start()

    def step(t):
        for at in range(4):
            for core in range(2):

                @pl.when((z == at) & (sec == core))
                def _():
                    step_at(t, at, core)

    def arrived(item):
        for core in range(2):

            @pl.when(sec == core)
            def _():
                copy(views(1 - core)[-1](item), 16, item, dev_core).wait_recv()

    def end():
        for b in range(per_layer):
            cross(b).wait_send()
        for core in range(2):

            @pl.when(sec == core)
            def _():
                _, own_a, col_a, eight_a, own_d, pair_d, eight_d, whole = views(core)
                every = slice(None)

                def sent(ref, kind):
                    copy(ref, kind, 0, dev_core).wait_send()

                sent(whole(every), 16)
                sent(col_a(every), 6)
                sent(eight_a(every), 7)
                sent(eight_d(every), 15)
                sent(own_d(every, 0), 8)
                for hop in (1, 2, 3):
                    for base, block in ((0, own_a), (9, pair_d)):

                        @pl.when((z < 3) & (z - (hop - 1) >= 0))
                        def _():
                            sent(block(every, 0), base + hop - 1)

                        @pl.when((z > 0) & (z + (hop - 1) <= 3))
                        def _():
                            sent(block(every, 0), base + 2 + hop)

    return begin, vec_here, step, arrived, end, dev_core, in_plane, along_z


def wide(ref, columns):
    block = ref[:, :, :, :, columns]
    return block.reshape(-1, block.shape[-1])


def dot_nt(left, right):
    return lax.dot_general(left, right, (((1,), (1,)), ((), ())), preferred_element_type=jnp.float32)


def dot_nn(left, right):
    return jnp.dot(left, right, preferred_element_type=jnp.float32)


def pair_bias(codes):
    down = jnp.broadcast_to(codes, (128, codes.shape[1])).T[:, :1]
    return jnp.where(down == codes, 0.0, -1000000000.0)


def lane_half(pair, half):
    lanes = lax.broadcasted_iota(jnp.int32, pair.shape, 1)
    return jnp.where((lanes < HEAD_DIM) == (half == 0), pair, jnp.zeros_like(pair))


def layers_kernel(with_links, *refs):
    if with_links:
        wq, wo, wi, wf, *refs = refs
    else:
        full, *refs = refs
    tokens, cotangent, segments, lengths, *refs = refs
    if with_links:
        parts, refs = refs[:7], refs[7:]
        full, *refs = refs
    else:
        given_vec, *refs = refs
    (y_out, grad_out, sums, prob_save, qkv_save, ctx_save, slope_save, norm_save, inv_save, *refs) = refs
    (x, vec, m_qkv, m_attn, m_hidden, m_final, qkv, ctx, hid, act, slope, acc, bias, probs, norms, invs, *refs) = refs
    (grad, proj_grad, layer_sums, in_sem, load_sem, p_sem, save_sem, m_sem, sem, out_sem, *refs) = refs
    sec = lax.axis_index("section")
    if with_links:
        (stage, got_core, got_plane, got_z, part_core, part_plane, *link_sems) = refs
        *link_sems, ex_send, ex_recv, sum_send, sum_recv = link_sems

    def start(copies):
        for copy in copies:
            copy.start()

    def wait(copies):
        for copy in copies:
            copy.wait()

    take_x = pltpu.make_async_copy(tokens.at[sec, 0], x, in_sem.at[0])
    take_grad = pltpu.make_async_copy(cotangent.at[sec, 0], grad, in_sem.at[1])
    take_x.start()
    take_grad.start()
    if with_links:
        bias_q, bias_v, bias_out, bias_in, bias_ffn_out, ln_gain, ln_shift = parts
        for k, ref in enumerate((bias_q, bias_v, bias_out)):
            vec[sec, k : k + 1, :] = ref[...]
        for k in range(4):
            vec[sec, 3 + k : 4 + k, :] = bias_in[:, k * LANES : (k + 1) * LANES]
        vec[sec, 7:8, :] = bias_ffn_out[...]
        vec[sec, 8:10, :] = ln_gain[0]
        vec[sec, 10:12, :] = ln_shift[0]
        vec[sec, 12:16, :] = jnp.zeros((4, LANES), jnp.float32)
        begin_links, vec_here, step_links, arrived, end_links, dev_core, in_plane, along_z = link_plan(
            wq, wo, wi, wf, full, vec, stage, *link_sems
        )
        begin_links()
    else:
        take_vec = pltpu.make_async_copy(given_vec, vec, in_sem.at[2])
        take_vec.start()
        take_vec.wait()
    valid = lax.broadcasted_iota(jnp.int32, (1, SEQ), 1) < lengths[sec, 0]
    bias[...] = pair_bias(segments[sec] * 2 + valid.astype(jnp.int32))
    take_x.wait()
    if with_links:
        vec_here()

    def row(layer, index):
        return vec[layer, index : index + 1, :]

    def hand_over(which, source, out, layer):
        local = pltpu.make_async_copy(source, out.at[sec], out_sem.at[which])
        if with_links:
            far = pltpu.make_async_remote_copy(
                src_ref=source,
                dst_ref=out.at[sec],
                send_sem=ex_send.at[which],
                recv_sem=ex_recv.at[which],
                device_id=dev_core,
                device_id_type=MESH,
            )
            return local, far
        return (pltpu.make_async_copy(source, out.at[layer], out_sem.at[which]),)

    def hand_start(which, source, out, layer):
        copies = hand_over(which, source, out, layer)
        if with_links:

            @pl.when(layer == sec)
            def _():
                copies[0].start()

            @pl.when(layer != sec)
            def _():
                copies[1].start()

        else:
            copies[0].start()

    def hand_wait(which, source, out, layer):
        copies = hand_over(which, source, out, layer)
        if with_links:

            @pl.when(layer == sec)
            def _():
                copies[0].wait()

            @pl.when(layer != sec)
            def _():
                copies[1].wait_send()

        else:
            copies[0].wait()

    def hand_arrived(which, source, out):
        pltpu.make_async_remote_copy(
            src_ref=source,
            dst_ref=out.at[1 - sec],
            send_sem=ex_send.at[which],
            recv_sem=ex_recv.at[which],
            device_id=dev_core,
            device_id_type=MESH,
        ).wait_recv()

    def load(item):
        b = item % PER_LAYER

        def into(b):
            if b < 3:
                return m_qkv.at[:, :, :, :, b * LANES : (b + 1) * LANES]
            if b == 3:
                return m_attn
            if b < 8:
                return m_hidden.at[:, :, :, :, (b - 4) * LANES : (b - 3) * LANES]
            return m_final.at[(b - 8) // 2, :, :, :, ((b - 8) % 2) * BLOCK : ((b - 8) % 2 + 1) * BLOCK, :]

        for k in range(PER_LAYER):

            @pl.when(b == k)
            def _():
                pltpu.make_async_copy(full.at[item], into(k), load_sem.at[k]).start()

    def loaded(b):
        pltpu.make_async_copy(full.at[0], m_attn, load_sem.at[b]).wait()

    def project(layer, b):
        scale = jnp.where(b == 0, 0.125, 1.0)
        shift = jnp.where(b == 0, row(layer, 0), jnp.where(b == 2, row(layer, 1), 0.0))
        at = pl.multiple_of(b * LANES, LANES)
        for n in range(0, LANES, TILE):
            columns = pl.ds(at + n, TILE)
            out = dot_nn(x[...], wide(m_qkv, columns)) + shift[:, n : n + TILE]
            qkv[:, columns] = (out.astype(jnp.bfloat16).astype(jnp.float32) * scale).astype(jnp.bfloat16)

    def save_p(layer, p):
        slot = p % 2
        return pltpu.make_async_copy(probs.at[slot], prob_save.at[layer, p], p_sem.at[slot])

    def attend(layer, first, last):
        def one(p, _):
            @pl.when(p >= 2)
            def _():
                save_p(layer, p).wait()

            at = pl.multiple_of(p * 128, 128)
            q, k, v = (qkv[:, pl.ds(part * LANES + at, 128)] for part in range(3))
            total = None
            for half in range(2):
                scores = dot_nt(lane_half(q, half), k) + bias[...]
                exps = jnp.exp(scores - jnp.max(scores, -1, keepdims=True))
                share = (exps / jnp.sum(exps, -1, keepdims=True)).astype(jnp.bfloat16)
                probs[p % 2, half] = share
                out = dot_nn(share, lane_half(v, half))
                total = out if total is None else total + out
            ctx[:, pl.ds(at, 128)] = total.astype(jnp.bfloat16)
            save_p(layer, p).start()
            return 0

        lax.fori_loop(first, last, one, 0)

    def save(which):
        pairs = (
            (qkv, qkv_save),
            (ctx, ctx_save),
            (slope, slope_save),
            (norms.at[0], norm_save.at[0]),
            (invs.at[0], inv_save.at[0]),
            (norms.at[1], norm_save.at[1]),
            (invs.at[1], inv_save.at[1]),
        )
        return pltpu.make_async_copy(*pairs[which], save_sem.at[which])

    def normalize(layer, which, put):
        for r in range(0, SEQ, 128):
            rows = slice(r, r + 128)
            residual = acc[rows, :]
            centered = residual - jnp.mean(residual, -1, keepdims=True)
            inverse = lax.rsqrt(jnp.mean(centered * centered, -1, keepdims=True) + epsilon)
            normed = centered * inverse
            norms[which, rows, :] = normed.astype(jnp.bfloat16)
            invs[which, rows, :] = jnp.broadcast_to(inverse, (128, 128))
            put[rows, :] = (normed * row(layer, 8 + which) + row(layer, 10 + which)).astype(jnp.bfloat16)

    def attn_out(layer):
        for n in range(0, LANES, TILE):
            columns = slice(n, n + TILE)
            acc[:, columns] = x[:, columns].astype(jnp.float32) + (
                dot_nn(ctx[...], wide(m_attn, columns)) + row(layer, 2)[:, columns]
            )
        normalize(layer, 0, hid)

    def ffn_in(layer, j):
        shift = vec[layer, pl.ds(3 + j, 1), :]
        at = pl.multiple_of(j * LANES, LANES)
        for n in range(0, LANES, TILE):
            pre = dot_nn(hid[...], wide(m_hidden, pl.ds(at + n, TILE))) + shift[:, n : n + TILE]
            cdf = 0.5 * (1.0 + lax.erf(pre * math.sqrt(0.5)))
            pdf = jnp.exp(pre * pre * -0.5) * (1.0 / math.sqrt(2.0 * math.pi))
            value = (pre * cdf).astype(jnp.bfloat16)
            grade = (cdf + pre * pdf).astype(jnp.bfloat16)
            to = pl.ds(pl.multiple_of(j * 512 + n // 2, 128), 128)
            for half in range(2):
                act[half, :, to] = value[:, half * 128 : (half + 1) * 128]
                slope[half, :, to] = grade[:, half * 128 : (half + 1) * 128]

    def ffn_out(layer, half):
        for n in range(0, LANES, TILE):
            columns = slice(n, n + TILE)
            out = dot_nn(act[half], wide(m_final.at[half], columns))
            if half == 0:
                acc[:, columns] = hid[:, columns].astype(jnp.float32) + (out + row(layer, 7)[:, columns])
            else:
                acc[:, columns] += out

    def compute(c):
        layer, b = c // PER_LAYER, c % PER_LAYER

        def lower(then):
            pl.when(layer == 0)(then)

        @pl.when(b <= 2)
        def _():
            loaded(b)

            @pl.when((b == 0) & (layer == 1))
            def _():
                wait([save(5), save(6)])

            project(layer, b)

        @pl.when(b == 2)
        def _():
            lower(lambda: start([save(0)]))
            attend(layer, 0, 2)

        @pl.when(b == 3)
        def _():
            loaded(3)
            attend(layer, 2, 5)

        @pl.when(b == 4)
        def _():
            loaded(4)
            attend(layer, 5, 8)

        @pl.when(b == 5)
        def _():
            lower(lambda: start([save(1)]))
            loaded(5)
            attn_out(layer)
            lower(lambda: start([save(3), save(4)]))

        @pl.when((b >= 5) & (b <= 8))
        def _():
            ffn_in(layer, b - 5)

        @pl.when(b == 6)
        def _():
            loaded(6)
            wait([save_p(layer, 0), save_p(layer, 1)])
            lower(lambda: wait([save(0), save(1)]))

        @pl.when(b == 7)
        def _():
            loaded(7)

        @pl.when(b == 8)
        def _():
            lower(lambda: start([save(2)]))
            loaded(8)

        @pl.when(b == 9)
        def _():
            loaded(9)

            @pl.when(layer == 1)
            def _():
                hand_wait(0, x, y_out, 0)

            ffn_out(layer, 0)
            lower(lambda: wait([save(3), save(4)]))

        @pl.when(b == 10)
        def _():
            loaded(10)
            lower(lambda: wait([save(2)]))

        @pl.when(b == 11)
        def _():
            loaded(11)
            ffn_out(layer, 1)
            normalize(layer, 1, x)
            lower(lambda: start([save(5), save(6)]))
            hand_start(layer, x, y_out, layer)

    def step(t, _):
        if with_links:
            step_links(t)
        first = t - LOAD

        @pl.when((first >= 0) & (first < ITEMS))
        def _():
            if with_links:
                arrived(first)
            load(first)

        second = t - LOAD - 1

        @pl.when((second >= 0) & (second < ITEMS))
        def _():
            compute(second)

        return 0

    lax.fori_loop(0, ITEMS + LOAD + 1, step, 0)
    def fetch_final(half):
        return [
            pltpu.make_async_copy(
                full.at[8 + 2 * half + g],
                m_final.at[half, :, :, :, g * BLOCK : (g + 1) * BLOCK, :],
                m_sem.at[2 * half + g],
            )
            for g in range(2)
        ]

    def fetch_hidden():
        return [
            pltpu.make_async_copy(
                full.at[4 + j], m_hidden.at[:, :, :, :, j * LANES : (j + 1) * LANES], m_sem.at[4 + j]
            )
            for j in range(4)
        ]

    def fetch_attn():
        return [pltpu.make_async_copy(full.at[3], m_attn, m_sem.at[8])]

    def fetch_qkv():
        return [
            pltpu.make_async_copy(full.at[j], m_qkv.at[:, :, :, :, j * LANES : (j + 1) * LANES], m_sem.at[9 + j])
            for j in range(3)
        ]

    def fetch_norm(which):
        return [
            pltpu.make_async_copy(norm_save.at[which], norms.at[which], sem.at[2 * which]),
            pltpu.make_async_copy(inv_save.at[which], invs.at[which], sem.at[2 * which + 1]),
        ]

    def fetch_slope(half):
        return [pltpu.make_async_copy(slope_save.at[half], slope.at[half], sem.at[4 + half])]

    def fetch_heads():
        return [
            pltpu.make_async_copy(qkv_save, qkv, sem.at[6]),
            pltpu.make_async_copy(ctx_save, ctx, sem.at[7]),
        ]

    def fetch_probs(layer, p):
        return [pltpu.make_async_copy(prob_save.at[layer, p], probs.at[p % 2], p_sem.at[p % 2])]

    start(fetch_probs(1, 0) + fetch_probs(1, 1))
    take_grad.wait()

    def column_sum(values):
        return jnp.sum(values.astype(jnp.float32), 0, keepdims=True)

    def norm_back(layer, which, upstream_of):
        gain = vec[layer, 8 + which : 9 + which, :]
        total = jnp.zeros((1, LANES), jnp.float32)
        for r in range(0, SEQ, 128):
            rows = slice(r, r + 128)
            upstream = upstream_of(rows) * gain
            normed = norms[which, rows, :].astype(jnp.float32)
            back = invs[which, rows, 0:1] * (
                upstream
                - jnp.mean(upstream, -1, keepdims=True)
                - normed * jnp.mean(upstream * normed, -1, keepdims=True)
            )
            acc[rows, :] = back
            low = back.astype(jnp.bfloat16)
            hid[rows, :] = low
            total = total + column_sum(low)
        return total

    def sum_copy(source, target, k, device):
        return pltpu.make_async_remote_copy(
            src_ref=source,
            dst_ref=target,
            send_sem=sum_send.at[k],
            recv_sem=sum_recv.at[k],
            device_id=device,
            device_id_type=MESH,
        )

    def core_sums():
        return [sum_copy(layer_sums.at[1 - sec], got_core, 0, dev_core)]

    def plane_sums():
        return [sum_copy(part_core, got_plane.at[k], 1 + k, device) for k, device in enumerate(in_plane)]

    def z_sums():
        return [sum_copy(part_plane, got_z.at[k], 4 + k, device) for k, device in enumerate(along_z)]

    def begin_sums():
        start(core_sums())

    def then_sums(k):
        if k == 0:
            wait(core_sums())
            part_core[...] = layer_sums[sec] + got_core[...]
            start(plane_sums())
        elif k == 1:
            wait(plane_sums())
            part_plane[...] = part_core[...] + (got_plane[0] + got_plane[1]) + got_plane[2]
            start(z_sums())
        elif k == 3:
            wait(z_sums())
            sums[...] = part_plane[...] + (got_z[0] + got_z[1]) + got_z[2]

    def one_layer(s, _):
        layer = 1 - s

        def prefetch(copies):
            @pl.when(s == 0)
            def _():
                start(copies)

        def fetched(copies):
            @pl.when(s == 1)
            def _():
                wait(copies)

        fetched(fetch_norm(1))
        layer_sums[layer, 7:8, :] = norm_back(layer, 1, lambda rows: grad[rows, :].astype(jnp.float32))
        prefetch(fetch_norm(1))
        for half in range(2):
            fetched(fetch_final(half) + fetch_slope(half))
            for n in range(0, 2048, TILE):
                chip = n // 128
                block = m_final[half, chip // 4, (chip // 2) % 2].reshape(TILE, LANES)
                back = dot_nt(hid[...], block) * slope[half, :, n : n + TILE].astype(jnp.float32)
                low = back.astype(jnp.bfloat16)
                total = column_sum(low)
                for k in range(2):
                    at = (chip + k) * 256 + half * 128
                    part = slice(k * 128, (k + 1) * 128)
                    act[at // 2048, :, at % 2048 : at % 2048 + 128] = low[:, part]
                    layer_sums[layer, 3 + at // LANES : 4 + at // LANES, at % LANES : at % LANES + 128] = total[:, part]
            prefetch(fetch_final(half) + fetch_slope(half))
        fetched(fetch_hidden())
        for n in range(0, LANES, TILE):
            block = m_hidden[n // TILE].reshape(TILE, 4 * LANES)
            acc[:, n : n + TILE] += dot_nt(act[0], block[:, : 2 * LANES]) + dot_nt(act[1], block[:, 2 * LANES :])
        prefetch(fetch_hidden())
        fetched(fetch_norm(0))
        layer_sums[layer, 2:3, :] = norm_back(
            layer, 0, lambda rows: acc[rows, :].astype(jnp.bfloat16).astype(jnp.float32)
        )
        prefetch(fetch_norm(0))

        @pl.when(s == 1)
        def _():
            hand_wait(3, grad, grad_out, 1)

        fetched(fetch_attn())
        for n in range(0, LANES, TILE):
            block = m_attn[n // TILE].reshape(TILE, LANES)
            grad[:, n : n + TILE] = dot_nt(hid[...], block).astype(jnp.bfloat16)
        prefetch(fetch_attn())
        fetched(fetch_heads())

        def one_pair(p, _):
            wait(fetch_probs(layer, p))
            at = pl.multiple_of(p * 128, 128)
            q, k, v = (qkv[:, pl.ds(part * LANES + at, 128)] for part in range(3))
            upper = grad[:, pl.ds(at, 128)]
            product = upper.astype(jnp.float32) * ctx[:, pl.ds(at, 128)].astype(jnp.float32)
            q_t, upper_t = q.T, upper.T
            grad_q = None
            grad_k, grad_v = [], []
            for half in range(2):
                weights = probs[p % 2, half]
                delta = jnp.sum(lane_half(product, half), -1, keepdims=True)
                scores = dot_nt(lane_half(upper, half), v)
                low = (weights.astype(jnp.float32) * (scores - delta)).astype(jnp.bfloat16)
                part = dot_nn(low, lane_half(k, half))
                grad_q = part if grad_q is None else grad_q + part
                here = slice(half * HEAD_DIM, (half + 1) * HEAD_DIM)
                grad_k.append(dot_nn(q_t[here], low))
                grad_v.append(dot_nn(upper_t[here], weights))
            back_q = (grad_q * 0.125).astype(jnp.bfloat16)
            back_v = jnp.concatenate(grad_v, 0).astype(jnp.bfloat16).T
            proj_grad[:, pl.ds(at, 128)] = back_q
            proj_grad[:, pl.ds(LANES + at, 128)] = jnp.concatenate(grad_k, 0).astype(jnp.bfloat16).T
            proj_grad[:, pl.ds(2 * LANES + at, 128)] = back_v
            layer_sums[layer, 0:1, pl.ds(at, 128)] = column_sum(back_q)
            layer_sums[layer, 1:2, pl.ds(at, 128)] = column_sum(back_v)

            @pl.when(p < 6)
            def _():
                start(fetch_probs(layer, p + 2))

            return 0

        lax.fori_loop(0, 8, one_pair, 0)
        prefetch(fetch_heads() + fetch_probs(0, 0) + fetch_probs(0, 1))
        fetched(fetch_qkv())

        def columns_of(n):
            block = m_qkv[n // TILE].reshape(TILE, 3 * LANES)
            columns = slice(n, n + TILE)
            grad[:, columns] = (acc[:, columns] + dot_nt(proj_grad[...], block)).astype(jnp.bfloat16)

        if with_links:

            @pl.when(s == 0)
            def _():
                for n in range(0, LANES, TILE):
                    columns_of(n)

            @pl.when(s == 1)
            def _():
                begin_sums()
                for k, n in enumerate(range(0, LANES, TILE)):
                    columns_of(n)
                    then_sums(k)

        else:
            for n in range(0, LANES, TILE):
                columns_of(n)
        prefetch(fetch_qkv())
        hand_start(2 + layer, grad, grad_out, layer)
        return 0

    lax.fori_loop(0, 2, one_layer, 0)
    hand_wait(1, x, y_out, 1)
    hand_wait(2, grad, grad_out, 0)
    if with_links:
        hand_arrived(sec, x, y_out)
        hand_arrived(2 + sec, grad, grad_out)
        end_links()
    else:
        sums[...] = layer_sums[...]


def both_layers(weights, tokens, cotangent, segments, lengths, vectors):
    with_links = len(weights) == 4
    low, wide_type = jnp.bfloat16, jnp.float32
    in_hbm = pl.BlockSpec(memory_space=pltpu.HBM)
    in_vmem = pl.BlockSpec(memory_space=pltpu.VMEM)
    in_smem = pl.BlockSpec(memory_space=pltpu.SMEM)
    shape = jax.ShapeDtypeStruct
    sums = (8, LANES) if with_links else (2, 8, LANES)
    outs = [shape((ITEMS, 4, 2, 2, BLOCK, LANES), low)] if with_links else []
    outs += [
        shape((2, SEQ, LANES), low),
        shape((2, SEQ, LANES), low),
        shape(sums, wide_type),
        shape((2, PAIRS, 2, SEQ, SEQ), low),
        shape((SEQ, 3 * LANES), low),
        shape((SEQ, LANES), low),
        shape((2, SEQ, 2 * LANES), low),
        shape((2, SEQ, LANES), low),
        shape((2, SEQ, 128), wide_type),
    ]
    out_specs = [in_hbm] * len(outs)
    out_specs[3 if with_links else 2] = in_vmem
    dma = pltpu.SemaphoreType.DMA
    scratch = [
        pltpu.VMEM((SEQ, LANES), low),
        pltpu.VMEM((2, 16, LANES), wide_type),
        pltpu.VMEM((4, 2, 2, BLOCK, 3 * LANES), low),
        pltpu.VMEM((4, 2, 2, BLOCK, LANES), low),
        pltpu.VMEM((4, 2, 2, BLOCK, 4 * LANES), low),
        pltpu.VMEM((2, 4, 2, 2, 2 * BLOCK, LANES), low),
        pltpu.VMEM((SEQ, 3 * LANES), low),
        pltpu.VMEM((SEQ, LANES), low),
        pltpu.VMEM((SEQ, LANES), low),
        pltpu.VMEM((2, SEQ, 2 * LANES), low),
        pltpu.VMEM((2, SEQ, 2 * LANES), low),
        pltpu.VMEM((SEQ, LANES), wide_type),
        pltpu.VMEM((SEQ, SEQ), wide_type),
        pltpu.VMEM((2, 2, SEQ, SEQ), low),
        pltpu.VMEM((2, SEQ, LANES), low),
        pltpu.VMEM((2, SEQ, 128), wide_type),
        pltpu.VMEM((SEQ, LANES), low),
        pltpu.VMEM((SEQ, 3 * LANES), low),
        pltpu.VMEM((2, 8, LANES), wide_type),
        dma((3,)),
        dma((PER_LAYER,)),
        dma((2,)),
        dma((7,)),
        dma((PER_LAYER,)),
        dma((8,)),
        dma((4,)),
    ]
    if with_links:
        specs = [in_hbm] * 6 + [in_vmem, in_smem] + [in_vmem] * 7
        scratch += [
            pltpu.VMEM((PER_LAYER, HALF, LANES), low),
            pltpu.VMEM((8, LANES), wide_type),
            pltpu.VMEM((3, 8, LANES), wide_type),
            pltpu.VMEM((3, 8, LANES), wide_type),
            pltpu.VMEM((8, LANES), wide_type),
            pltpu.VMEM((8, LANES), wide_type),
            dma((PER_LAYER,)),
            dma((PER_LAYER,)),
            dma((PER_LAYER,)),
            dma((PER_LAYER,)),
            dma((17,)),
            dma((17, ITEMS)),
            dma((2,)),
            dma((4,)),
            dma((4,)),
            dma((7,)),
            dma((7,)),
        ]
        params = pltpu.CompilerParams(collective_id=0, has_side_effects=True, vmem_limit_bytes=VMEM_LIMIT)
    else:
        specs = [in_hbm] * 3 + [in_vmem, in_smem, in_hbm]
        params = pltpu.CompilerParams(vmem_limit_bytes=VMEM_LIMIT)
    results = pl.pallas_call(
        partial(layers_kernel, with_links),
        out_shape=tuple(outs),
        in_specs=specs,
        out_specs=tuple(out_specs),
        scratch_shapes=scratch,
        compiler_params=params,
    )(*weights, tokens, cotangent, segments, lengths, *vectors)
    return results[1:4] if with_links else results[:3]


def gather(w_qkv, w_out, w_in, w_ffn_out):
    matrices = [lax.all_gather(w[0], "dp", axis=0, tiled=True) for w in (w_qkv, w_out, w_in, w_ffn_out)]
    qkv, attn, hidden, final = matrices
    blocks = [qkv[:, b * LANES : (b + 1) * LANES] for b in range(3)] + [attn]
    blocks += [hidden[:, b * LANES : (b + 1) * LANES] for b in range(4)]
    final = final.reshape(16, 4, BLOCK, LANES).transpose(1, 0, 2, 3).reshape(4, 1024, LANES)
    own = jnp.concatenate([jnp.stack(blocks), final])
    return lax.all_gather(own, "section", axis=0, tiled=True).reshape(24, 4, 2, 2, BLOCK, LANES)


def on_device(
    tokens,
    segment_ids,
    row_lengths,
    w_qkv,
    w_out,
    w_in,
    w_ffn_out,
    bias_q,
    bias_v,
    bias_out,
    bias_in,
    bias_ffn_out,
    ln_gain,
    ln_shift,
    out_cotangent,
):
    weights = (w_qkv, w_out, w_in, w_ffn_out)
    vectors = (bias_q, bias_v, bias_out, bias_in, bias_ffn_out, ln_gain, ln_shift)
    data = (tokens, out_cotangent, segment_ids, row_lengths)
    if w_qkv.shape[1] == BLOCK:
        tops, grads, sums = both_layers(weights, *data, vectors)
    else:
        sec = lax.axis_index("section")
        wide_in, gains, shifts = bias_in.reshape(4, LANES), ln_gain[0], ln_shift[0]
        vec = jnp.concatenate(
            [bias_q, bias_v, bias_out, wide_in, bias_ffn_out, gains, shifts, jnp.zeros((4, LANES))]
        )
        vec = lax.all_gather(vec, "section", axis=0)
        tops, grads, sums = both_layers((gather(*weights),), *data, (vec,))

        def swap(array):
            return lax.ppermute(array, "section", [(0, 1), (1, 0)])

        def placed(both):
            got = swap(jnp.where(sec == 0, both[1], both[0]))
            return jnp.where(sec == 0, jnp.stack([both[0], got]), jnp.stack([got, both[1]]))

        tops, grads = placed(tops), placed(grads)
        sums = jnp.where(sec == 0, sums[0], sums[1]) + swap(jnp.where(sec == 0, sums[1], sums[0]))
        sums = lax.psum(sums, "dp")
    totals = (sums[0:1], sums[1:2], sums[2:3], sums[3:7].reshape(1, 4 * LANES), sums[7:8])
    return (tops[None, :, None], grads[None, :, None]) + totals


def solution(mesh):
    placed = (
        P(None, "dp", None, None),
        P(None, "dp", None),
        P(None, "dp"),
        P("section", "dp", None),
        P("section", "dp", None),
        P("section", "dp", None),
        P("section", "dp", None),
        P("section", None),
        P("section", None),
        P("section", None),
        P("section", None),
        P("section", None),
        P("section", None, None),
        P("section", None, None),
        P(None, "dp", None, None),
    )
    return jax.shard_map(
        on_device,
        mesh=mesh,
        in_specs=placed,
        out_specs=(
            P("section", None, "dp", None, None),
            P("section", None, "dp", None, None),
            P("section", None),
            P("section", None),
            P("section", None),
            P("section", None),
            P("section", None),
        ),
        check_vma=False,
    )
```

time: 367 us -> 279 us (0.76)
  blocking collectives: 74.8 us -> 0 us
  other arithmetic: 13.7 us -> 0 us
  local copies, waits for them, and re-layouts: 4.51 us -> 8.79 us
    psum x1 -> x0, blocking collectives: 74.8 us -> none  [on_device(): sums = lax.psum(sums, 'dp')]
    select_n x3 -> x0, other arithmetic: 6.58 us -> none  [the longest x2 6.57 us: placed(): jnp.where(sec == 0, jnp.stack([both[0], got]), jnp.stack([got, both[1]]))]
    unnamed x9 -> x7, local copies, waits for them, and re-layouts: 1.16 us -> 7.23 us
    another operation x2 -> x0, other arithmetic: 4.39 us -> none  [placed(): jnp.stack([got, both[1]])]
    pallas_call x2 -> x1, Pallas kernels: 270 us -> 269 us  [both_layers(): pl.pallas_call(partial(layers_kernel, with_links), out_shape=tuple(outs),...]
  transfers between devices with their start and end apart: 3 -> 0, of which waited for: 1 -> 0; matrix products, arithmetic and copies ran while one was open for 2% -> 0% of each run, Pallas kernels for 0% -> 0%
where the time goes in v2:
time: 279 us; the launch traced here: 278 us
  Pallas kernels  269 us (96%)
  local copies, waits for them, and re-layouts  8.79 us (3%)
    pallas_call x1, Pallas kernels, both_layers(): pl.pallas_call(partial(layers_kernel, with_links), out_shape=tuple(outs),...  269 us
    unnamed x7, local copies, waits for them, and re-layouts  7.23 us

profile of v2, /device:TPU:0, one launch (start us, length us, event | category | flops | bytes accessed | tf_op | source)
XLA Modules:
  0.0 278.3 jit_solution(6625144093060404579)
XLA Ops:
  0.6 1.3 copy.22.refs_7_
  1.9 268.9 %shard_map.198 = (bf16[24,4,2,2,64,1024]{5,4,3,2,1,0:T(8,128)(2,1)}, bf16[2,512,1024]{2,1,0:T(8,128)(2,1)}, bf16[2,512,1024]{2,1,0:T(8,128)(2,1)}, f32[8,1024]{1...) custom-call(bf16[1,64,3072]{2,1,0:T(8,128)(2,1)} %refs_0_.1, ...), custom_call_target="tpu_custom_call" | custom-call | tf_op jit(solution)/shard_map/pallas_call | solution.py:928
  270.8 0.8 slice_bitcast_fusion
  271.6 1.6 fusion
  273.1 0.6 copy.25
  273.8 0.0 copy-start
  273.8 3.2 %copy.28 = bf16[1,2,1,512,1024]{4,3,2,1,0:T(8,128)(2,1)} copy(bf16[1,2,1,512,1024]{4,3,2,1,0:T(8,128)(2,1)} %bitcast.11) | data formatting | bytes 4194304
  277.0 0.0 copy-done
  277.0 1.3 copy.29
Async XLA Ops:
  273.8 3.2 %copy-start = (bf16[2,512,1024]{2,1,0:T(8,128)(2,1)S(1)}, bf16[2,512,1024]{2,1,0:T(8,128)(2,1)}, u32[]{:S(2)}) copy-start(bf16[2,512,1024]{2,1,0:T(8,128)(2,1)} %get-tuple-element.11) | copy-start | bytes 6291460

commit v3 on v2

--- a/solution.py
+++ b/solution.py
@@ -10,7 +10,7 @@
 
 HEAD_DIM = 64
 SEQ = 512
-PAIRS = 8
+GROUPS = 4
 epsilon = 1e-06
 VMEM_LIMIT = 60 * 2**20
 MESH = pl.DeviceIdType.MESH
@@ -22,7 +22,8 @@
 CUT = 384
 STAGES = (1, 2, 3, 4, 6)
 LOAD = 7
-FRONT = 2
+FRONT = 6
+SETTLE = 3
 TILE = 256
 
 
@@ -86,9 +87,10 @@
         for b in range(per_layer):
             to_stage(b).start()
         barrier = pltpu.get_barrier_semaphore()
-        for device in (dev_core, *in_plane, *along_z):
+        for k in range(1, 32):
+            device = ((sec + k // 16) % 2, (chip + k) % 16)
             pl.semaphore_signal(barrier, inc=1, device_id=device, device_id_type=MESH)
-        pl.semaphore_wait(barrier, 7)
+        pl.semaphore_wait(barrier, 31)
         for b in range(per_layer):
             cross(b).start()
         give_vec(vec.at[sec]).start()
@@ -176,11 +178,14 @@
                         device_id_type=MESH,
                     ).wait_recv()
 
-                z_send(0, own_a, 1, item, at)
                 copy(own_d(item, at), 8, item, dev_v).start()
 
         for lead in range(FRONT):
             first_move(t * FRONT + lead)
+
+        @pl.when(live(t))
+        def _():
+            z_send(0, own_a, 1, t, at)
 
         item1 = turns[0]
 
@@ -309,11 +314,11 @@
         given_vec, *refs = refs
     (y_out, grad_out, sums, prob_save, qkv_save, ctx_save, slope_save, norm_save, inv_save, *refs) = refs
     (x, vec, m_qkv, m_attn, m_hidden, m_final, qkv, ctx, hid, act, slope, acc, bias, probs, norms, invs, *refs) = refs
-    (grad, proj_grad, layer_sums, in_sem, load_sem, p_sem, save_sem, m_sem, sem, out_sem, *refs) = refs
+    (grad, proj_grad, layer_sums, head_sums, in_sem, load_sem, p_sem, save_sem, m_sem, sem, out_sem, *refs) = refs
     sec = lax.axis_index("section")
     if with_links:
-        (stage, got_core, got_plane, got_z, part_core, part_plane, *link_sems) = refs
-        *link_sems, ex_send, ex_recv, sum_send, sum_recv = link_sems
+        (stage, got_core, got_plane, got_z, got_late, part_core, part_plane, *link_sems) = refs
+        *link_sems, ex_send, ex_recv, sum_send, sum_recv, late_sent, late_got = link_sems
 
     def start(copies):
         for copy in copies:
@@ -327,6 +332,7 @@
     take_grad = pltpu.make_async_copy(cotangent.at[sec, 0], grad, in_sem.at[1])
     take_x.start()
     take_grad.start()
+    head_sums[...] = jnp.zeros_like(head_sums)
     if with_links:
         bias_q, bias_v, bias_out, bias_in, bias_ffn_out, ln_gain, ln_shift = parts
         for k, ref in enumerate((bias_q, bias_v, bias_out)):
@@ -344,12 +350,15 @@
     else:
         take_vec = pltpu.make_async_copy(given_vec, vec, in_sem.at[2])
         take_vec.start()
-        take_vec.wait()
-    valid = lax.broadcasted_iota(jnp.int32, (1, SEQ), 1) < lengths[sec, 0]
-    bias[...] = pair_bias(segments[sec] * 2 + valid.astype(jnp.int32))
-    take_x.wait()
-    if with_links:
-        vec_here()
+
+    def settle():
+        valid = lax.broadcasted_iota(jnp.int32, (1, SEQ), 1) < lengths[0, sec]
+        bias[...] = pair_bias(segments[sec] * 2 + valid.astype(jnp.int32))
+        take_x.wait()
+        if with_links:
+            vec_here()
+        else:
+            take_vec.wait()
 
     def row(layer, index):
         return vec[layer, index : index + 1, :]
@@ -439,14 +448,14 @@
             qkv[:, columns] = (out.astype(jnp.bfloat16).astype(jnp.float32) * scale).astype(jnp.bfloat16)
 
     def save_p(layer, p):
-        slot = p % 2
-        return pltpu.make_async_copy(probs.at[slot], prob_save.at[layer, p], p_sem.at[slot])
+        group, k = p // 2, p % 2
+        return pltpu.make_async_copy(probs.at[group % 2, k], prob_save.at[layer, group, k], p_sem.at[p % 4])
 
     def attend(layer, first, last):
         def one(p, _):
-            @pl.when(p >= 2)
-            def _():
-                save_p(layer, p).wait()
+            @pl.when(p >= 4)
+            def _():
+                save_p(layer, p - 4).wait()
 
             at = pl.multiple_of(p * 128, 128)
             q, k, v = (qkv[:, pl.ds(part * LANES + at, 128)] for part in range(3))
@@ -455,7 +464,7 @@
                 scores = dot_nt(lane_half(q, half), k) + bias[...]
                 exps = jnp.exp(scores - jnp.max(scores, -1, keepdims=True))
                 share = (exps / jnp.sum(exps, -1, keepdims=True)).astype(jnp.bfloat16)
-                probs[p % 2, half] = share
+                probs[(p // 2) % 2, p % 2, half] = share
                 out = dot_nn(share, lane_half(v, half))
                 total = out if total is None else total + out
             ctx[:, pl.ds(at, 128)] = total.astype(jnp.bfloat16)
@@ -563,7 +572,7 @@
         @pl.when(b == 6)
         def _():
             loaded(6)
-            wait([save_p(layer, 0), save_p(layer, 1)])
+            wait([save_p(layer, p) for p in range(4, 8)])
             lower(lambda: wait([save(0), save(1)]))
 
         @pl.when(b == 7)
@@ -602,6 +611,11 @@
     def step(t, _):
         if with_links:
             step_links(t)
+
+        @pl.when(t == SETTLE)
+        def _():
+            settle()
+
         first = t - LOAD
 
         @pl.when((first >= 0) & (first < ITEMS))
@@ -661,8 +675,8 @@
             pltpu.make_async_copy(ctx_save, ctx, sem.at[7]),
         ]
 
-    def fetch_probs(layer, p):
-        return [pltpu.make_async_copy(prob_save.at[layer, p], probs.at[p % 2], p_sem.at[p % 2])]
+    def fetch_probs(layer, group):
+        return [pltpu.make_async_copy(prob_save.at[layer, group], probs.at[group % 2], p_sem.at[group % 2])]
 
     start(fetch_probs(1, 0) + fetch_probs(1, 1))
     take_grad.wait()
@@ -698,6 +712,12 @@
             device_id_type=MESH,
         )
 
+    def spread_heads(target, where, group, heads):
+        for row in range(2):
+            for k in range(2):
+                at = (2 * group + k) * 128
+                target[where, row : row + 1, at : at + 128] = heads[2 * row + k : 2 * row + k + 1, :]
+
     def core_sums():
         return [sum_copy(layer_sums.at[1 - sec], got_core, 0, dev_core)]
 
@@ -707,21 +727,74 @@
     def z_sums():
         return [sum_copy(part_plane, got_z.at[k], 4 + k, device) for k, device in enumerate(along_z)]
 
-    def begin_sums():
+    def begin_early():
+        layer_sums[0, 0:2, :] = jnp.zeros((2, LANES), jnp.float32)
+        for group in range(GROUPS):
+            spread_heads(layer_sums, 1, group, head_sums[1, group])
         start(core_sums())
 
-    def then_sums(k):
-        if k == 0:
+    def early_sums(k):
+        @pl.when(k == 0)
+        def _():
             wait(core_sums())
             part_core[...] = layer_sums[sec] + got_core[...]
             start(plane_sums())
-        elif k == 1:
+
+        @pl.when(k == 2)
+        def _():
             wait(plane_sums())
             part_plane[...] = part_core[...] + (got_plane[0] + got_plane[1]) + got_plane[2]
             start(z_sums())
-        elif k == 3:
-            wait(z_sums())
-            sums[...] = part_plane[...] + (got_z[0] + got_z[1]) + got_z[2]
+
+    def end_early():
+        wait(z_sums())
+        sums[0] = part_plane[...] + (got_z[0] + got_z[1]) + got_z[2]
+
+    def late_send(group):
+        own = 16 * sec + lax.axis_index("dp")
+        got_late[group, own] = head_sums[0, group]
+
+        def one(k, _):
+            sum_late(group, own, (0, (lax.axis_index("dp") + k) % 16)).start()
+            return 0
+
+        lax.fori_loop(1, 16, one, 0)
+
+        @pl.when(sec == 1)
+        def _():
+            sum_late(group, own, dev_core).start()
+
+    def sum_late(group, slot, device):
+        return pltpu.make_async_remote_copy(
+            src_ref=head_sums.at[0, group],
+            dst_ref=got_late.at[group, slot],
+            send_sem=late_sent.at[group],
+            recv_sem=late_got.at[group],
+            device_id=device,
+            device_id_type=MESH,
+        )
+
+    def end_late():
+        def many(group, count):
+            several = got_late.at[group, pl.ds(0, count)]
+            return pltpu.make_async_remote_copy(
+                src_ref=several,
+                dst_ref=several,
+                send_sem=late_sent.at[group],
+                recv_sem=late_got.at[group],
+                device_id=dev_core,
+                device_id_type=MESH,
+            )
+
+        for group in range(GROUPS):
+            for core in range(2):
+
+                @pl.when(sec == core)
+                def _():
+                    many(group, 15 + core).wait_send()
+                    if core == 0:
+                        many(group, 31).wait_recv()
+                        spread_heads(sums, 0, group, jnp.sum(got_late[group], 0))
 
     def one_layer(s, _):
         layer = 1 - s
@@ -775,40 +848,53 @@
         prefetch(fetch_attn())
         fetched(fetch_heads())
 
-        def one_pair(p, _):
-            wait(fetch_probs(layer, p))
+        def one_group(group, _):
+            wait(fetch_probs(layer, group))
+            for k in range(2):
+                one_pair(2 * group + k, group, k, probs.at[group % 2, k])
+
+            @pl.when(group < GROUPS - 2)
+            def _():
+                start(fetch_probs(layer, group + 2))
+
+            if with_links:
+
+                @pl.when(s == 1)
+                def _():
+                    late_send(group)
+                    early_sums(group)
+
+            return 0
+
+        def one_pair(p, group, k, shares):
             at = pl.multiple_of(p * 128, 128)
-            q, k, v = (qkv[:, pl.ds(part * LANES + at, 128)] for part in range(3))
+            q, keys, v = (qkv[:, pl.ds(part * LANES + at, 128)] for part in range(3))
             upper = grad[:, pl.ds(at, 128)]
             product = upper.astype(jnp.float32) * ctx[:, pl.ds(at, 128)].astype(jnp.float32)
-            q_t, upper_t = q.T, upper.T
-            grad_q = None
-            grad_k, grad_v = [], []
+            q_t, k_t, upper_t = q.T, keys.T, upper.T
+            grad_q, grad_k, grad_v = [], [], []
             for half in range(2):
-                weights = probs[p % 2, half]
+                weights = shares[half]
                 delta = jnp.sum(lane_half(product, half), -1, keepdims=True)
                 scores = dot_nt(lane_half(upper, half), v)
                 low = (weights.astype(jnp.float32) * (scores - delta)).astype(jnp.bfloat16)
-                part = dot_nn(low, lane_half(k, half))
-                grad_q = part if grad_q is None else grad_q + part
                 here = slice(half * HEAD_DIM, (half + 1) * HEAD_DIM)
+                grad_q.append(dot_nt(k_t[here], low) * 0.125)
                 grad_k.append(dot_nn(q_t[here], low))
                 grad_v.append(dot_nn(upper_t[here], weights))
-            back_q = (grad_q * 0.125).astype(jnp.bfloat16)
-            back_v = jnp.concatenate(grad_v, 0).astype(jnp.bfloat16).T
-            proj_grad[:, pl.ds(at, 128)] = back_q
-            proj_grad[:, pl.ds(LANES + at, 128)] = jnp.concatenate(grad_k, 0).astype(jnp.bfloat16).T
-            proj_grad[:, pl.ds(2 * LANES + at, 128)] = back_v
-            layer_sums[layer, 0:1, pl.ds(at, 128)] = column_sum(back_q)
-            layer_sums[layer, 1:2, pl.ds(at, 128)] = column_sum(back_v)
-
-            @pl.when(p < 6)
-            def _():
-                start(fetch_probs(layer, p + 2))
-
-            return 0
-
-        lax.fori_loop(0, 8, one_pair, 0)
+            for part, rows in enumerate((grad_q, grad_k, grad_v)):
+                back = jnp.concatenate(rows, 0).astype(jnp.bfloat16).T
+                proj_grad[:, pl.ds(part * LANES + at, 128)] = back
+                if part != 1:
+                    head_sums[layer, group, part + k : part + k + 1, :] = column_sum(back)
+
+        if with_links:
+
+            @pl.when(s == 1)
+            def _():
+                begin_early()
+
+        lax.fori_loop(0, GROUPS, one_group, 0)
         prefetch(fetch_heads() + fetch_probs(0, 0) + fetch_probs(0, 1))
         fetched(fetch_qkv())
 
@@ -826,10 +912,11 @@
 
             @pl.when(s == 1)
             def _():
-                begin_sums()
-                for k, n in enumerate(range(0, LANES, TILE)):
+                for n in range(0, LANES, TILE):
                     columns_of(n)
-                    then_sums(k)
+                    if n == TILE:
+                        end_early()
+                end_late()
 
         else:
             for n in range(0, LANES, TILE):
@@ -846,6 +933,9 @@
         hand_arrived(2 + sec, grad, grad_out)
         end_links()
     else:
+        for layer in range(2):
+            for group in range(GROUPS):
+                spread_heads(layer_sums, layer, group, head_sums[layer, group])
         sums[...] = layer_sums[...]
 
 
@@ -856,13 +946,13 @@
     in_vmem = pl.BlockSpec(memory_space=pltpu.VMEM)
     in_smem = pl.BlockSpec(memory_space=pltpu.SMEM)
     shape = jax.ShapeDtypeStruct
-    sums = (8, LANES) if with_links else (2, 8, LANES)
+    sums = (1, 8, LANES) if with_links else (2, 8, LANES)
     outs = [shape((ITEMS, 4, 2, 2, BLOCK, LANES), low)] if with_links else []
     outs += [
         shape((2, SEQ, LANES), low),
         shape((2, SEQ, LANES), low),
         shape(sums, wide_type),
-        shape((2, PAIRS, 2, SEQ, SEQ), low),
+        shape((2, GROUPS, 2, 2, SEQ, SEQ), low),
         shape((SEQ, 3 * LANES), low),
         shape((SEQ, LANES), low),
         shape((2, SEQ, 2 * LANES), low),
@@ -886,15 +976,16 @@
         pltpu.VMEM((2, SEQ, 2 * LANES), low),
         pltpu.VMEM((SEQ, LANES), wide_type),
         pltpu.VMEM((SEQ, SEQ), wide_type),
-        pltpu.VMEM((2, 2, SEQ, SEQ), low),
+        pltpu.VMEM((2, 2, 2, SEQ, SEQ), low),
         pltpu.VMEM((2, SEQ, LANES), low),
         pltpu.VMEM((2, SEQ, 128), wide_type),
         pltpu.VMEM((SEQ, LANES), low),
         pltpu.VMEM((SEQ, 3 * LANES), low),
         pltpu.VMEM((2, 8, LANES), wide_type),
+        pltpu.VMEM((2, GROUPS, 8, 128), wide_type),
         dma((3,)),
         dma((PER_LAYER,)),
-        dma((2,)),
+        dma((4,)),
         dma((7,)),
         dma((PER_LAYER,)),
         dma((8,)),
@@ -907,6 +998,7 @@
             pltpu.VMEM((8, LANES), wide_type),
             pltpu.VMEM((3, 8, LANES), wide_type),
             pltpu.VMEM((3, 8, LANES), wide_type),
+            pltpu.VMEM((GROUPS, 32, 8, 128), wide_type),
             pltpu.VMEM((8, LANES), wide_type),
             pltpu.VMEM((8, LANES), wide_type),
             dma((PER_LAYER,)),
@@ -920,6 +1012,8 @@
             dma((4,)),
             dma((7,)),
             dma((7,)),
+            dma((GROUPS,)),
+            dma((GROUPS,)),
         ]
         params = pltpu.CompilerParams(collective_id=0, has_side_effects=True, vmem_limit_bytes=VMEM_LIMIT)
     else:
@@ -965,9 +1059,10 @@
 ):
     weights = (w_qkv, w_out, w_in, w_ffn_out)
     vectors = (bias_q, bias_v, bias_out, bias_in, bias_ffn_out, ln_gain, ln_shift)
-    data = (tokens, out_cotangent, segment_ids, row_lengths)
+    data = (tokens, out_cotangent, segment_ids, row_lengths.T)
     if w_qkv.shape[1] == BLOCK:
         tops, grads, sums = both_layers(weights, *data, vectors)
+        sums = sums[0]
     else:
         sec = lax.axis_index("section")
         wide_in, gains, shifts = bias_in.reshape(4, LANES), ln_gain[0], ln_shift[0]

time: 279 us -> 271 us (0.971)
  Pallas kernels: 269 us -> 263 us
    pallas_call x1, Pallas kernels: 269 us -> 263 us  [both_layers(): pl.pallas_call(partial(layers_kernel, with_links), out_shape=tuple(outs),...]
    unnamed x7 -> x6, local copies, waits for them, and re-layouts: 7.23 us -> 5.94 us
where the time goes in v3:
time: 271 us
  Pallas kernels  263 us (97%)
  local copies, waits for them, and re-layouts  7.49 us (3%)
    pallas_call x1, Pallas kernels, both_layers(): pl.pallas_call(partial(layers_kernel, with_links), out_shape=tuple(outs),...  263 us
    unnamed x6, local copies, waits for them, and re-layouts  5.94 us

profile of v3, /device:TPU:0, one launch (start us, length us, event | category | flops | bytes accessed | tf_op | source)
XLA Modules:
  0.0 270.7 jit_solution(7892965513836341580)
XLA Ops:
  0.6 262.6 %shard_map.198 = (bf16[24,4,2,2,64,1024]{5,4,3,2,1,0:T(8,128)(2,1)}, bf16[2,512,1024]{2,1,0:T(8,128)(2,1)}, bf16[2,512,1024]{2,1,0:T(8,128)(2,1)}, f32[1,8,1024]...) custom-call(bf16[1,64,3072]{2,1,0:T(8,128)(2,1)} %refs_0_.1, ...), custom_call_target="tpu_custom_call" | custom-call | tf_op jit(solution)/shard_map/pallas_call | solution.py:1022
  263.2 0.8 slice_bitcast_fusion
  264.0 1.6 slice_bitcast_fusion.1
  265.5 0.6 copy.24
  266.2 0.0 copy-start
  266.2 3.2 %copy.27 = bf16[1,2,1,512,1024]{4,3,2,1,0:T(8,128)(2,1)} copy(bf16[1,2,1,512,1024]{4,3,2,1,0:T(8,128)(2,1)} %bitcast.19) | data formatting | bytes 4194304
  269.4 0.0 copy-done
  269.4 1.3 copy.28
Async XLA Ops:
  266.2 3.2 %copy-start = (bf16[2,512,1024]{2,1,0:T(8,128)(2,1)S(1)}, bf16[2,512,1024]{2,1,0:T(8,128)(2,1)}, u32[]{:S(2)}) copy-start(bf16[2,512,1024]{2,1,0:T(8,128)(2,1)} %get-tuple-element.11) | copy-start | bytes 6291460

commit v4 on v3

--- a/solution.py
+++ b/solution.py
@@ -12,7 +12,7 @@
 SEQ = 512
 GROUPS = 4
 epsilon = 1e-06
-VMEM_LIMIT = 60 * 2**20
+VMEM_LIMIT = 58 * 2**20
 MESH = pl.DeviceIdType.MESH
 ITEMS = 24
 PER_LAYER = ITEMS // 2
@@ -50,28 +50,48 @@
             return wo.at[0, pl.ds(row, HALF), :]
         if b < 8:
             return wi.at[0, pl.ds(row, HALF), (b - 4) * LANES : (b - 3) * LANES]
-        return wf.at[0, pl.ds((b - 8) * BLOCK + row, HALF), :]
+        pair, columns = (b - 8) // 2, slice((b % 2) * 512, (b % 2) * 512 + 512)
+        return [wf.at[0, pl.ds((2 * pair + g) * BLOCK + row, HALF), columns] for g in range(2)]
 
     mine = pl.multiple_of(sec * HALF, HALF)
     other = pl.multiple_of((1 - sec) * HALF, HALF)
 
     def to_stage(b):
-        return pltpu.make_async_copy(own_block(b, mine), stage.at[b], in_sem.at[b])
+        return pltpu.make_async_copy(stage.at[b], stage.at[b], in_sem.at[b])
+
+    def stage_start(b):
+        block = own_block(b, mine)
+        if b < 8:
+            pltpu.make_async_copy(block, stage.at[b], in_sem.at[b]).start()
+        else:
+            for g in range(2):
+                pltpu.make_async_copy(block[g], stage.at[b, :, g * 512 : (g + 1) * 512], in_sem.at[b]).start()
 
     def to_place(b):
         return pltpu.make_async_copy(
             stage.at[b], full.at[sec * per_layer + b, z, y, x, pl.ds(mine, HALF), :], place_sem.at[b]
         )
 
-    def cross(b):
+    def cross_copy(b, source, columns):
         return pltpu.make_async_remote_copy(
-            src_ref=own_block(b, other),
-            dst_ref=full.at[sec * per_layer + b, z, y, x, pl.ds(other, HALF), :],
+            src_ref=source,
+            dst_ref=full.at[sec * per_layer + b, z, y, x, pl.ds(other, HALF), columns],
             send_sem=cross_send.at[b],
             recv_sem=cross_recv.at[b],
             device_id=dev_core,
             device_id_type=MESH,
         )
+
+    def cross_start(b):
+        block = own_block(b, other)
+        if b < 8:
+            cross_copy(b, block, slice(None)).start()
+        else:
+            for g in range(2):
+                cross_copy(b, block[g], slice(g * 512, (g + 1) * 512)).start()
+
+    def cross_sent(b):
+        cross_copy(b, stage.at[b], slice(None)).wait_send()
 
     def give_vec(where):
         return pltpu.make_async_remote_copy(
@@ -85,14 +105,14 @@
 
     def begin():
         for b in range(per_layer):
-            to_stage(b).start()
+            stage_start(b)
         barrier = pltpu.get_barrier_semaphore()
         for k in range(1, 32):
             device = ((sec + k // 16) % 2, (chip + k) % 16)
             pl.semaphore_signal(barrier, inc=1, device_id=device, device_id_type=MESH)
         pl.semaphore_wait(barrier, 31)
         for b in range(per_layer):
-            cross(b).start()
+            cross_start(b)
         give_vec(vec.at[sec]).start()
         for b in range(per_layer):
             to_stage(b).wait()
@@ -248,7 +268,7 @@
 
     def end():
         for b in range(per_layer):
-            cross(b).wait_send()
+            cross_sent(b)
         for core in range(2):
 
             @pl.when(sec == core)
@@ -314,7 +334,7 @@
         given_vec, *refs = refs
     (y_out, grad_out, sums, prob_save, qkv_save, ctx_save, slope_save, norm_save, inv_save, *refs) = refs
     (x, vec, m_qkv, m_attn, m_hidden, m_final, qkv, ctx, hid, act, slope, acc, bias, probs, norms, invs, *refs) = refs
-    (grad, proj_grad, layer_sums, head_sums, in_sem, load_sem, p_sem, save_sem, m_sem, sem, out_sem, *refs) = refs
+    (grad, layer_sums, head_sums, in_sem, load_sem, p_sem, save_sem, m_sem, sem, out_sem, *refs) = refs
     sec = lax.axis_index("section")
     if with_links:
         (stage, got_core, got_plane, got_z, got_late, part_core, part_plane, *link_sems) = refs
@@ -427,13 +447,25 @@
                 return m_attn
             if b < 8:
                 return m_hidden.at[:, :, :, :, (b - 4) * LANES : (b - 3) * LANES]
-            return m_final.at[(b - 8) // 2, :, :, :, ((b - 8) % 2) * BLOCK : ((b - 8) % 2 + 1) * BLOCK, :]
+            return None
 
         for k in range(PER_LAYER):
 
             @pl.when(b == k)
             def _():
-                pltpu.make_async_copy(full.at[item], into(k), load_sem.at[k]).start()
+                if k < 8:
+                    pltpu.make_async_copy(full.at[item], into(k), load_sem.at[k]).start()
+                else:
+                    for g in range(2):
+                        final_part(item, k, g, load_sem.at[k]).start()
+
+    def final_part(item, b, g, semaphore):
+        columns = slice((b % 2) * 512, (b % 2) * 512 + 512)
+        return pltpu.make_async_copy(
+            full.at[item, :, :, :, :, g * 512 : (g + 1) * 512],
+            m_final.at[(b - 8) // 2, :, :, :, g * BLOCK : (g + 1) * BLOCK, columns],
+            semaphore,
+        )
 
     def loaded(b):
         pltpu.make_async_copy(full.at[0], m_attn, load_sem.at[b]).wait()
@@ -518,8 +550,8 @@
                 act[half, :, to] = value[:, half * 128 : (half + 1) * 128]
                 slope[half, :, to] = grade[:, half * 128 : (half + 1) * 128]
 
-    def ffn_out(layer, half):
-        for n in range(0, LANES, TILE):
+    def ffn_out(layer, half, part):
+        for n in range(part * 512, part * 512 + 512, TILE):
             columns = slice(n, n + TILE)
             out = dot_nn(act[half], wide(m_final.at[half], columns))
             if half == 0:
@@ -592,18 +624,20 @@
             def _():
                 hand_wait(0, x, y_out, 0)
 
-            ffn_out(layer, 0)
+            ffn_out(layer, 0, 0)
+            ffn_out(layer, 0, 1)
             lower(lambda: wait([save(3), save(4)]))
 
         @pl.when(b == 10)
         def _():
             loaded(10)
+            ffn_out(layer, 1, 0)
             lower(lambda: wait([save(2)]))
 
         @pl.when(b == 11)
         def _():
             loaded(11)
-            ffn_out(layer, 1)
+            ffn_out(layer, 1, 1)
             normalize(layer, 1, x)
             lower(lambda: start([save(5), save(6)]))
             hand_start(layer, x, y_out, layer)
@@ -635,11 +669,8 @@
     lax.fori_loop(0, ITEMS + LOAD + 1, step, 0)
     def fetch_final(half):
         return [
-            pltpu.make_async_copy(
-                full.at[8 + 2 * half + g],
-                m_final.at[half, :, :, :, g * BLOCK : (g + 1) * BLOCK, :],
-                m_sem.at[2 * half + g],
-            )
+            final_part(8 + 2 * half + k, 8 + 2 * half + k, g, m_sem.at[(0, 12)[half] + 2 * k + g])
+            for k in range(2)
             for g in range(2)
         ]
 
@@ -884,7 +915,7 @@
                 grad_v.append(dot_nn(upper_t[here], weights))
             for part, rows in enumerate((grad_q, grad_k, grad_v)):
                 back = jnp.concatenate(rows, 0).astype(jnp.bfloat16).T
-                proj_grad[:, pl.ds(part * LANES + at, 128)] = back
+                act[part // 2, :, pl.ds((part % 2) * LANES + at, 128)] = back
                 if part != 1:
                     head_sums[layer, group, part + k : part + k + 1, :] = column_sum(back)
 
@@ -901,7 +932,8 @@
         def columns_of(n):
             block = m_qkv[n // TILE].reshape(TILE, 3 * LANES)
             columns = slice(n, n + TILE)
-            grad[:, columns] = (acc[:, columns] + dot_nt(proj_grad[...], block)).astype(jnp.bfloat16)
+            total = dot_nt(act[0], block[:, : 2 * LANES]) + dot_nt(act[1, :, :LANES], block[:, 2 * LANES :])
+            grad[:, columns] = (acc[:, columns] + total).astype(jnp.bfloat16)
 
         if with_links:
 
@@ -949,8 +981,8 @@
     sums = (1, 8, LANES) if with_links else (2, 8, LANES)
     outs = [shape((ITEMS, 4, 2, 2, BLOCK, LANES), low)] if with_links else []
     outs += [
-        shape((2, SEQ, LANES), low),
-        shape((2, SEQ, LANES), low),
+        pltpu.VMEM((2, SEQ, LANES), low),
+        pltpu.VMEM((2, SEQ, LANES), low),
         shape(sums, wide_type),
         shape((2, GROUPS, 2, 2, SEQ, SEQ), low),
         shape((SEQ, 3 * LANES), low),
@@ -960,7 +992,8 @@
         shape((2, SEQ, 128), wide_type),
     ]
     out_specs = [in_hbm] * len(outs)
-    out_specs[3 if with_links else 2] = in_vmem
+    for k in range(3):
+        out_specs[k + with_links] = in_vmem
     dma = pltpu.SemaphoreType.DMA
     scratch = [
         pltpu.VMEM((SEQ, LANES), low),
@@ -980,14 +1013,13 @@
         pltpu.VMEM((2, SEQ, LANES), low),
         pltpu.VMEM((2, SEQ, 128), wide_type),
         pltpu.VMEM((SEQ, LANES), low),
-        pltpu.VMEM((SEQ, 3 * LANES), low),
         pltpu.VMEM((2, 8, LANES), wide_type),
         pltpu.VMEM((2, GROUPS, 8, 128), wide_type),
         dma((3,)),
         dma((PER_LAYER,)),
         dma((4,)),
         dma((7,)),
-        dma((PER_LAYER,)),
+        dma((16,)),
         dma((8,)),
         dma((4,)),
     ]
@@ -1035,7 +1067,7 @@
     qkv, attn, hidden, final = matrices
     blocks = [qkv[:, b * LANES : (b + 1) * LANES] for b in range(3)] + [attn]
     blocks += [hidden[:, b * LANES : (b + 1) * LANES] for b in range(4)]
-    final = final.reshape(16, 4, BLOCK, LANES).transpose(1, 0, 2, 3).reshape(4, 1024, LANES)
+    final = final.reshape(16, 2, 2, BLOCK, 2, 512).transpose(1, 4, 0, 3, 2, 5).reshape(4, 1024, LANES)
     own = jnp.concatenate([jnp.stack(blocks), final])
     return lax.all_gather(own, "section", axis=0, tiled=True).reshape(24, 4, 2, 2, BLOCK, LANES)
 

time: 271 us -> 266 us (0.982)
  local copies, waits for them, and re-layouts: 7.49 us -> 3.89 us
where the time goes in v4:
time: 266 us
  Pallas kernels  262 us (98%)
  local copies, waits for them, and re-layouts  3.89 us (1%)
    pallas_call x1, Pallas kernels, both_layers(): pl.pallas_call(partial(layers_kernel, with_links), out_shape=tuple(outs),...  262 us

profile of v4, /device:TPU:0, one launch (start us, length us, event | category | flops | bytes accessed | tf_op | source)
XLA Modules:
  0.0 266.1 jit_solution(9003298880358223721)
XLA Ops:
  0.6 261.6 %shard_map.198 = (bf16[24,4,2,2,64,1024]{5,4,3,2,1,0:T(8,128)(2,1)}, bf16[2,512,1024]{2,1,0:T(8,128)(2,1)S(1)}, bf16[2,512,1024]{2,1,0:T(8,128)(2,1)S(1)}, f32[1...) custom-call(bf16[1,64,3072]{2,1,0:T(8,128)(2,1)} %refs_0_.1, ...), custom_call_target="tpu_custom_call" | custom-call | tf_op jit(solution)/shard_map/pallas_call | solution.py:1054
  262.2 1.3 copy.27
  263.6 0.0 copy-start
  263.6 1.3 copy.28
  264.9 0.0 copy-done
  264.9 0.6 slice_bitcast_fusion.1
  265.5 0.6 copy.24
  (1 shorter events, 0.0 us)
Async XLA Ops:
  263.6 1.3 copy-start

commit v5 on v4

--- a/solution.py
+++ b/solution.py
@@ -517,8 +517,8 @@
         )
         return pltpu.make_async_copy(*pairs[which], save_sem.at[which])
 
-    def normalize(layer, which, put):
-        for r in range(0, SEQ, 128):
+    def normalize(layer, which, put, first=0, last=SEQ):
+        for r in range(first, last, 128):
             rows = slice(r, r + 128)
             residual = acc[rows, :]
             centered = residual - jnp.mean(residual, -1, keepdims=True)
@@ -550,14 +550,14 @@
                 act[half, :, to] = value[:, half * 128 : (half + 1) * 128]
                 slope[half, :, to] = grade[:, half * 128 : (half + 1) * 128]
 
-    def ffn_out(layer, half, part):
+    def ffn_out(layer, half, part, rows=slice(0, SEQ)):
         for n in range(part * 512, part * 512 + 512, TILE):
             columns = slice(n, n + TILE)
-            out = dot_nn(act[half], wide(m_final.at[half], columns))
+            out = dot_nn(act[half, rows], wide(m_final.at[half], columns))
             if half == 0:
-                acc[:, columns] = hid[:, columns].astype(jnp.float32) + (out + row(layer, 7)[:, columns])
+                acc[rows, columns] = hid[rows, columns].astype(jnp.float32) + (out + row(layer, 7)[:, columns])
             else:
-                acc[:, columns] += out
+                acc[rows, columns] += out
 
     def compute(c):
         layer, b = c // PER_LAYER, c % PER_LAYER
@@ -637,8 +637,9 @@
         @pl.when(b == 11)
         def _():
             loaded(11)
-            ffn_out(layer, 1, 1)
-            normalize(layer, 1, x)
+            for top in (0, SEQ // 2):
+                ffn_out(layer, 1, 1, slice(top, top + SEQ // 2))
+                normalize(layer, 1, x, top, top + SEQ // 2)
             lower(lambda: start([save(5), save(6)]))
             hand_start(layer, x, y_out, layer)
 
@@ -715,10 +716,10 @@
     def column_sum(values):
         return jnp.sum(values.astype(jnp.float32), 0, keepdims=True)
 
-    def norm_back(layer, which, upstream_of):
+    def norm_back(layer, which, upstream_of, first=0, last=SEQ):
         gain = vec[layer, 8 + which : 9 + which, :]
         total = jnp.zeros((1, LANES), jnp.float32)
-        for r in range(0, SEQ, 128):
+        for r in range(first, last, 128):
             rows = slice(r, r + 128)
             upstream = upstream_of(rows) * gain
             normed = norms[which, rows, :].astype(jnp.float32)
@@ -840,11 +841,10 @@
             def _():
                 wait(copies)
 
-        fetched(fetch_norm(1))
+        fetched(fetch_norm(1) + fetch_final(0) + fetch_slope(0) + fetch_final(1) + fetch_slope(1))
+        fetched(fetch_hidden() + fetch_norm(0) + fetch_attn())
         layer_sums[layer, 7:8, :] = norm_back(layer, 1, lambda rows: grad[rows, :].astype(jnp.float32))
-        prefetch(fetch_norm(1))
         for half in range(2):
-            fetched(fetch_final(half) + fetch_slope(half))
             for n in range(0, 2048, TILE):
                 chip = n // 128
                 block = m_final[half, chip // 4, (chip // 2) % 2].reshape(TILE, LANES)
@@ -856,27 +856,28 @@
                     part = slice(k * 128, (k + 1) * 128)
                     act[at // 2048, :, at % 2048 : at % 2048 + 128] = low[:, part]
                     layer_sums[layer, 3 + at // LANES : 4 + at // LANES, at % LANES : at % LANES + 128] = total[:, part]
-            prefetch(fetch_final(half) + fetch_slope(half))
-        fetched(fetch_hidden())
-        for n in range(0, LANES, TILE):
-            block = m_hidden[n // TILE].reshape(TILE, 4 * LANES)
-            acc[:, n : n + TILE] += dot_nt(act[0], block[:, : 2 * LANES]) + dot_nt(act[1], block[:, 2 * LANES :])
-        prefetch(fetch_hidden())
-        fetched(fetch_norm(0))
-        layer_sums[layer, 2:3, :] = norm_back(
-            layer, 0, lambda rows: acc[rows, :].astype(jnp.bfloat16).astype(jnp.float32)
-        )
-        prefetch(fetch_norm(0))
+        prefetch(fetch_norm(1) + fetch_final(0) + fetch_slope(0) + fetch_final(1) + fetch_slope(1))
 
         @pl.when(s == 1)
         def _():
             hand_wait(3, grad, grad_out, 1)
 
-        fetched(fetch_attn())
+        total = jnp.zeros((1, LANES), jnp.float32)
+        for top in (0, SEQ // 2):
+            rows = slice(top, top + SEQ // 2)
+            for n in range(0, LANES, TILE):
+                block = m_hidden[n // TILE].reshape(TILE, 4 * LANES)
+                acc[rows, n : n + TILE] += dot_nt(act[0, rows], block[:, : 2 * LANES]) + dot_nt(
+                    act[1, rows], block[:, 2 * LANES :]
+                )
+            total = total + norm_back(
+                layer, 0, lambda at: acc[at, :].astype(jnp.bfloat16).astype(jnp.float32), top, top + SEQ // 2
+            )
+        layer_sums[layer, 2:3, :] = total
         for n in range(0, LANES, TILE):
             block = m_attn[n // TILE].reshape(TILE, LANES)
             grad[:, n : n + TILE] = dot_nt(hid[...], block).astype(jnp.bfloat16)
-        prefetch(fetch_attn())
+        prefetch(fetch_hidden() + fetch_norm(0) + fetch_attn())
         fetched(fetch_heads())
 
         def one_group(group, _):

time: 266 us -> 264 us (level)
  Pallas kernels: 262 us -> 259 us
where the time goes in v5:
time: 264 us
  Pallas kernels  259 us (98%)
  local copies, waits for them, and re-layouts  3.89 us (1%)
    pallas_call x1, Pallas kernels, both_layers(): pl.pallas_call(partial(layers_kernel, with_links), out_shape=tuple(outs),...  259 us

profile of v5, /device:TPU:0, one launch (start us, length us, event | category | flops | bytes accessed | tf_op | source)
XLA Modules:
  0.0 263.8 jit_solution(11588779492523690937)
XLA Ops:
  0.6 259.3 %shard_map.198 = (bf16[24,4,2,2,64,1024]{5,4,3,2,1,0:T(8,128)(2,1)}, bf16[2,512,1024]{2,1,0:T(8,128)(2,1)S(1)}, bf16[2,512,1024]{2,1,0:T(8,128)(2,1)S(1)}, f32[1...) custom-call(bf16[1,64,3072]{2,1,0:T(8,128)(2,1)} %refs_0_.1, ...), custom_call_target="tpu_custom_call" | custom-call | tf_op jit(solution)/shard_map/pallas_call | solution.py:1055
  259.9 1.3 copy.27
  261.3 0.0 copy-start
  261.3 1.3 copy.28
  262.6 0.0 copy-done
  262.6 0.6 slice_bitcast_fusion.1
  263.2 0.6 copy.24
  (1 shorter events, 0.0 us)
Async XLA Ops:
  261.3 1.3 copy-start

commit v6 on v5

--- a/solution.py
+++ b/solution.py
@@ -20,8 +20,8 @@
 BLOCK = 64
 HALF = BLOCK // 2
 CUT = 384
-STAGES = (1, 2, 3, 4, 6)
-LOAD = 7
+STAGES = (1, 2, 3, 4, 5)
+LOAD = 6
 FRONT = 6
 SETTLE = 3
 TILE = 256

time: 264 us -> 264 us (level)
  no operation moved by 1% of the time
where the time goes in v6:
time: 264 us
  Pallas kernels  259 us (98%)
  local copies, waits for them, and re-layouts  3.89 us (1%)
    pallas_call x1, Pallas kernels, both_layers(): pl.pallas_call(partial(layers_kernel, with_links), out_shape=tuple(outs),...  259 us

profile of v6, /device:TPU:0, one launch (start us, length us, event | category | flops | bytes accessed | tf_op | source)
XLA Modules:
  0.0 263.8 jit_solution(15868316670226511680)
XLA Ops:
  0.6 259.3 %shard_map.198 = (bf16[24,4,2,2,64,1024]{5,4,3,2,1,0:T(8,128)(2,1)}, bf16[2,512,1024]{2,1,0:T(8,128)(2,1)S(1)}, bf16[2,512,1024]{2,1,0:T(8,128)(2,1)S(1)}, f32[1...) custom-call(bf16[1,64,3072]{2,1,0:T(8,128)(2,1)} %refs_0_.1, ...), custom_call_target="tpu_custom_call" | custom-call | tf_op jit(solution)/shard_map/pallas_call | solution.py:1055
  259.9 1.3 copy.27
  261.2 0.0 copy-start
  261.2 1.3 copy.28
  262.6 0.0 copy-done
  262.6 0.6 slice_bitcast_fusion.1
  263.2 0.6 copy.24
  (1 shorter events, 0.0 us)
Async XLA Ops:
  261.2 1.3 copy-start
